TPU v7x, 256 devices: a whole 4x4x8 slice. The times are simulated.
256 devices in a mesh: ctx: 16 (over x_hi, z), head: 16 (over y, x_lo, core).
Axes of the slice: x: 4 (x_hi: 2, x_lo: 2; x = x_hi * 2 + x_lo), y: 4, z: 8, core: 2. Of those that a mesh axis runs over, the one named last changes fastest.
Arguments:
- queries: bfloat16 [6144, 32, 128], P('ctx', 'head'), may hold values from -72 to 72
- codes: int32 [6144, 128], P('ctx'), may hold values from 0 to 255
- codebook_k: bfloat16 [8, 256, 128], replicated, may hold values from -6 to 6
- codebook_v: bfloat16 [8, 256, 128], replicated, may hold values from -6 to 6
- grad_out: bfloat16 [6144, 32, 128], P('ctx', 'head'), may hold values from -12 to 12
Outputs:
- attention: bfloat16 [6144, 32, 128], P('ctx', 'head')
- query_grad: bfloat16 [6144, 32, 128], P('ctx', 'head')
- book_grad_k: float32 [8, 256, 128], P(None, 'ctx', 'head')
- book_grad_v: float32 [8, 256, 128], P(None, 'ctx', 'head')
All inputs are finite; a program needn't handle non-finite values.
Results may differ from a plain program's by a relative error of at most 0.04.
Values may be sent and summed in bfloat16 or wider, within the bound.
No kernel may reach another device: no remote copies, remote signals or barrier semaphores. Data moves between devices by JAX's collectives and lax.ppermute only.
A program may use at most 64 MiB of HBM per device.

v0:
```python
import jax
import jax.numpy as jnp
from jax import lax
from jax.sharding import PartitionSpec as P

KVH = 8
HD = 128
SUB = 16
CODES = 256
GROUP = 4


NEGATIVE = -1e30


def block_rows(total_rows):
    chosen = 1
    for candidate in range(1, min(total_rows, 512) + 1):
        if total_rows % candidate == 0:
            chosen = candidate
    return chosen


def over_blocks(carried, members, first_row, step_fn):
    total_rows = members[0].shape[0]
    block_size = block_rows(total_rows)
    block_count = total_rows // block_size
    shaped = tuple(
        (member.reshape((block_count, block_size) + member.shape[1:]) for member in members)
    )

    def advance(running, element):
        block_index, parts_now = element
        return (step_fn(running, parts_now, first_row + block_index * block_size), None)

    result, unused = lax.scan(advance, carried, (jnp.arange(block_count, dtype=jnp.int32), shaped))
    return result


def causal_mask(query_first, query_rows, key_first, key_rows):
    query_positions = query_first + lax.iota(jnp.int32, query_rows)
    key_positions = key_first + lax.iota(jnp.int32, key_rows)
    return key_positions[None, :] <= query_positions[:, None]


def decode_rows(code_cols, books):
    row_count = code_cols.shape[0]
    kv_count, code_count, columns = books.shape
    sub_count = code_cols.shape[1] // kv_count
    levels = lax.broadcasted_iota(jnp.int32, (1, 1, code_count), 2)
    onehot = (
        (code_cols[:, :, None] == levels)
        .astype(jnp.bfloat16)
        .reshape(row_count, kv_count, sub_count, code_count)
    )
    tables = books.reshape(kv_count, code_count, sub_count, columns // sub_count)
    decoded = jnp.einsum("nhsc,hcsj->nhsj", onehot, tables, preferred_element_type=jnp.float32)
    return decoded.reshape(row_count, kv_count, columns).astype(jnp.bfloat16)


def code_sums(code_cols, gradient):
    row_count, kv_count, columns = gradient.shape
    sub_count = code_cols.shape[1] // kv_count
    levels = lax.broadcasted_iota(jnp.int32, (1, 1, CODES), 2)
    onehot = (
        (code_cols[:, :, None] == levels)
        .astype(jnp.float32)
        .reshape(row_count, kv_count, sub_count, CODES)
    )
    tables = gradient.reshape(row_count, kv_count, sub_count, columns // sub_count)
    summed = jnp.einsum(
        "nhsc,nhsj->hcsj",
        onehot,
        tables,
        precision=lax.Precision.HIGHEST,
        preferred_element_type=jnp.float32,
    )
    return summed.reshape(kv_count, CODES, columns)


def forward_step(running, key_rows, values, key_first, queries, query_first, group_loc):
    highest, weight_sum, accumulated = running
    expanded_key_rows = jnp.repeat(key_rows, group_loc, axis=1)
    expanded_value_rows = jnp.repeat(values, group_loc, axis=1)
    scores = jnp.einsum(
        "nhd,rhd->hnr", queries, expanded_key_rows, preferred_element_type=jnp.float32
    ) * HD ** (-0.5)
    allowed = causal_mask(query_first, queries.shape[0], key_first, key_rows.shape[0])
    scores = jnp.where(allowed[None], scores, NEGATIVE)
    new_highest = jnp.maximum(highest, jnp.max(scores, axis=2))
    attention_weight_matrix = jnp.where(
        allowed[None], jnp.exp(scores - new_highest[:, :, None]), 0.0
    )
    factor = jnp.exp(highest - new_highest)
    weight_sum = weight_sum * factor + jnp.sum(attention_weight_matrix, axis=2)
    accumulated = accumulated * factor.T[:, :, None] + jnp.einsum(
        "hnr,rhd->nhd",
        attention_weight_matrix.astype(jnp.bfloat16),
        expanded_value_rows,
        preferred_element_type=jnp.float32,
    )
    return (new_highest, weight_sum, accumulated)


def query_grad_step(
    running,
    key_rows,
    values,
    key_first,
    queries,
    douts,
    log_heads,
    fix_heads,
    query_first,
    group_loc,
):
    expanded_key_rows = jnp.repeat(key_rows, group_loc, axis=1)
    expanded_value_rows = jnp.repeat(values, group_loc, axis=1)
    scores = jnp.einsum(
        "nhd,rhd->hnr", queries, expanded_key_rows, preferred_element_type=jnp.float32
    ) * HD ** (-0.5)
    allowed = causal_mask(query_first, queries.shape[0], key_first, key_rows.shape[0])
    scores = jnp.where(allowed[None], scores, NEGATIVE)
    attention_weight_matrix = jnp.where(allowed[None], jnp.exp(scores - log_heads[:, :, None]), 0.0)
    products = jnp.einsum(
        "nhd,rhd->hnr", douts, expanded_value_rows, preferred_element_type=jnp.float32
    )
    linear_bias_slopes = (attention_weight_matrix * (products - fix_heads[:, :, None])).astype(
        jnp.bfloat16
    )
    return running + jnp.einsum(
        "hnr,rhd->nhd", linear_bias_slopes, expanded_key_rows, preferred_element_type=jnp.float32
    ) * HD ** (-0.5)


def key_grad_step(
    running,
    members,
    query_first,
    all_logs,
    all_fixes,
    key_rows,
    values,
    key_first,
    group_loc,
    kv_count,
):
    query_subspace_slice, output_gradient_subspace = members
    subspace_row_list = query_subspace_slice.shape[0]
    log_rows = lax.dynamic_slice_in_dim(all_logs, query_first, subspace_row_list, 0)
    fix_rows = lax.dynamic_slice_in_dim(all_fixes, query_first, subspace_row_list, 0)
    grad_keys, grad_values = running
    expanded_key_rows = jnp.repeat(key_rows, group_loc, axis=1)
    expanded_value_rows = jnp.repeat(values, group_loc, axis=1)
    scores = jnp.einsum(
        "fbz,ybz->bfy", query_subspace_slice, expanded_key_rows, preferred_element_type=jnp.float32
    ) * HD ** (-0.5)
    allowed = causal_mask(query_first, subspace_row_list, key_first, key_rows.shape[0])
    scores = jnp.where(allowed[None], scores, NEGATIVE)
    attention_weight_matrix = jnp.where(
        allowed[None], jnp.exp(scores - log_rows.T[:, :, None]), 0.0
    )
    value_terms = jnp.einsum(
        "auk,uaf->kaf",
        attention_weight_matrix.astype(jnp.bfloat16),
        output_gradient_subspace,
        preferred_element_type=jnp.float32,
    )
    products = jnp.einsum(
        "fbz,ybz->bfy",
        output_gradient_subspace,
        expanded_value_rows,
        preferred_element_type=jnp.float32,
    )
    linear_bias_slopes = (attention_weight_matrix * (products - fix_rows.T[:, :, None])).astype(
        jnp.bfloat16
    )
    key_terms = jnp.einsum(
        "auk,uaf->kaf", linear_bias_slopes, query_subspace_slice, preferred_element_type=jnp.float32
    ) * HD ** (-0.5)
    row_count = key_rows.shape[0]
    key_terms = jnp.sum(key_terms.reshape(row_count, kv_count, group_loc, HD), axis=2)
    value_terms = jnp.sum(value_terms.reshape(row_count, kv_count, group_loc, HD), axis=2)
    return (grad_keys + key_terms, grad_values + value_terms)


def per_device(queries, codes, codebook_k, codebook_v, grad_out):
    row_count, head_count, columns = queries.shape
    group_loc = min(head_count, GROUP)
    kv_count = max(1, head_count // GROUP)
    first_kv = lax.axis_index("head") * head_count // GROUP
    own_first = lax.axis_index("ctx") * row_count
    own_codes = lax.dynamic_slice_in_dim(codes, first_kv * SUB, kv_count * SUB, 1)
    books_k = lax.dynamic_slice_in_dim(codebook_k, first_kv, kv_count, 0)
    books_v = lax.dynamic_slice_in_dim(codebook_v, first_kv, kv_count, 0)
    own_keys = decode_rows(own_codes, books_k)
    own_values = decode_rows(own_codes, books_v)
    start_state = (
        jnp.full((head_count, row_count), NEGATIVE, jnp.float32),
        jnp.zeros((head_count, row_count), jnp.float32),
        jnp.zeros((row_count, head_count, columns), jnp.float32),
    )

    def forward_members(running, members, key_first):
        return forward_step(
            running, members[0], members[1], key_first, queries, own_first, group_loc
        )

    highest, weight_sum, accumulated = over_blocks(
        start_state,
        (
            lax.all_gather(own_keys, "ctx", axis=0, tiled=True),
            lax.all_gather(own_values, "ctx", axis=0, tiled=True),
        ),
        jnp.int32(0),
        forward_members,
    )
    attention = (accumulated / weight_sum.T[:, :, None]).astype(jnp.bfloat16)
    log_heads = highest + jnp.log(weight_sum)
    fix_heads = jnp.sum(grad_out.astype(jnp.float32) * attention.astype(jnp.float32), axis=2).T
    zero_grad = jnp.zeros((row_count, head_count, columns), jnp.float32)

    def grad_members(running, members, key_first):
        return query_grad_step(
            running,
            members[0],
            members[1],
            key_first,
            queries,
            grad_out,
            log_heads,
            fix_heads,
            own_first,
            group_loc,
        )

    grad_total = over_blocks(
        zero_grad,
        (
            lax.all_gather(own_keys, "ctx", axis=0, tiled=True),
            lax.all_gather(own_values, "ctx", axis=0, tiled=True),
        ),
        jnp.int32(0),
        grad_members,
    )
    all_logs, all_fixes = (
        lax.all_gather(log_heads.T, "ctx", axis=0, tiled=True),
        lax.all_gather(fix_heads.T, "ctx", axis=0, tiled=True),
    )

    def key_members(running, members, query_first):
        return key_grad_step(
            running,
            members,
            query_first,
            all_logs,
            all_fixes,
            own_keys,
            own_values,
            own_first,
            group_loc,
            kv_count,
        )

    zero_keys = jnp.zeros((row_count, kv_count, columns), jnp.float32)
    grad_keys, grad_values = over_blocks(
        (zero_keys, zero_keys),
        (
            lax.all_gather(queries, "ctx", axis=0, tiled=True),
            lax.all_gather(grad_out, "ctx", axis=0, tiled=True),
        ),
        jnp.int32(0),
        key_members,
    )
    book_terms = jnp.stack([code_sums(own_codes, grad_keys), code_sums(own_codes, grad_values)])
    padded = jnp.zeros((2, KVH, CODES, columns), jnp.float32)
    padded = lax.dynamic_update_slice_in_dim(padded, book_terms, first_kv, 1)
    by_column = lax.psum_scatter(
        padded.astype(jnp.bfloat16), "head", scatter_dimension=3, tiled=True
    )
    finished = lax.psum_scatter(by_column, "ctx", scatter_dimension=2, tiled=True).astype(
        jnp.float32
    )
    return (attention, grad_total.astype(jnp.bfloat16), finished[0], finished[1])


def solution(mesh):
    placed = (P("ctx", "head", None), P("ctx", None), P(), P(), P("ctx", "head", None))
    return jax.shard_map(
        per_device,
        mesh=mesh,
        in_specs=placed,
        out_specs=(
            P("ctx", "head", None),
            P("ctx", "head", None),
            P(None, "ctx", "head"),
            P(None, "ctx", "head"),
        ),
        check_vma=False,
    )
```

profile of v0, /device:TPU:1, one launch (start us, length us, event | category | flops | bytes accessed | tf_op | source)
XLA Modules:
  0.0 682.4 jit_solution(14942847252354253821)
XLA Ops:
  9.3 1.7 fusion.71
  12.0 1.7 fusion.70
  16.2 78.3 %all-gather.5.cloned.1.call-done = bf16[6144,1,128]{2,0,1:T(8,128)(2,1)} async-done(((bf16[384,1,128]{2,0,1:T(8,128)(2,1)}), bf16[6144,1,128]{2,0,1:T(8,128)(2,1)}) %all-gather.5.cloned.1.call-update) | async-done | bytes 1572880 | tf_op jit(solution)/shard_map/all_gather | solution.py:212
  94.5 81.5 %all-gather.7.cloned.1.call-done = bf16[6144,1,128]{2,0,1:T(8,128)(2,1)} async-done(((bf16[384,1,128]{2,0,1:T(8,128)(2,1)}), bf16[6144,1,128]{2,0,1:T(8,128)(2,1)}) %all-gather.7.cloned.1.call-update) | async-done | bytes 1572880 | tf_op jit(solution)/shard_map/all_gather | solution.py:213
  176.0 68.3 %while.39 = (s32[]{:T(128)}, f32[2,384]{1,0:T(2,128)S(1)}, f32[2,384]{1,0:T(2,128)S(1)}, f32[384,2,128]{0,2,1:T(8,128)S(1)}, s32[12]{0:T(128)S(1)}, /*index=5*/s...) while((s32[]{:T(128)}, f32[2,384]{1,0:T(2,128)S(1)}, ...), condition=%wide.region_3.4_spmd.clone, body=%wide.region_0.3_spmd.clone.sunk | while | flops 205362560 | bytes 7593137 | solution.py:36
  246.5 64.6 %all_gather.25 = f32[6144,2]{1,0:T(8,128)S(1)} all-gather(f32[384,2]{1,0:T(8,128)S(1)} %get-tuple-element.410), channel_id=1, replica_groups=mesh['ctx'=16,'head'=16] {'ctx'}, dimensions={0}, use_global_device_ids=true | all-gather | bytes 52224 | tf_op jit(solution)/shard_map/all_gather | solution.py:248
  311.1 1.8 copy.77
  312.9 30.7 %all_gather.23 = f32[6144,2]{0,1:T(2,128)S(1)} all-gather(f32[384,2]{0,1:T(2,128)S(1)} %bitcast.219), channel_id=1, replica_groups=mesh['ctx'=16,'head'=16] {'ctx'}, dimensions={0}, use_global_device_ids=true | all-gather | bytes 52224 | tf_op jit(solution)/shard_map/all_gather | solution.py:247
  343.6 26.0 %all-gather.11.cloned.1.call-done = bf16[6144,2,128]{2,0,1:T(8,128)(2,1)} async-done(((bf16[384,2,128]{2,0,1:T(8,128)(2,1)}), bf16[6144,2,128]{2,0,1:T(8,128)(2,1)}) %all-gather.11.cloned.1.call-update) | async-done | bytes 3145744 | tf_op jit(solution)/shard_map/all_gather | solution.py:270
  369.6 84.3 %while.41 = (s32[]{:T(128)}, f32[384,1,128]{0,2,1:T(8,128)}, f32[384,1,128]{2,0,1:T(8,128)S(1)}, bf16[12,512,2,128]{3,1,0,2:T(8,128)(2,1)}, s32[]{:T(128)}, /*in...) while((s32[]{:T(128)}, f32[384,1,128]{0,2,1:T(8,128)}, ...), condition=%wide.region_9.10_spmd.clone, body=%wide.region_7.9_spmd.clone.sunk | while | flops 406340480 | bytes 9535810 | solution.py:36
  380.4 1.7 fusion.127
  387.4 1.7 fusion.127
  394.4 1.7 fusion.127
  401.4 1.7 fusion.127
  408.5 1.7 fusion.127
  436.6 1.7 fusion.127
  443.6 1.7 fusion.127
  450.6 1.7 fusion.127
  454.0 2.6 fusion.69
  456.6 2.6 fusion.68
  460.7 60.9 %reduce-scatter.7.cloned.1.call-done = bf16[8,4096]{1,0:T(8,128)(2,1)} async-done(((bf16[128,4096]{1,0:T(8,128)(2,1)}), bf16[8,4096]{1,0:T(8,128)(2,1)}) %reduce-scatter.7.cloned.1.call-update) | async-done | bytes 65552
  523.5 1.7 reshape.258
  525.2 57.2 %while.40 = (s32[]{:T(128)}, f32[384,2,128]{0,2,1:T(8,128)S(1)}, bf16[12,512,1,128]{3,1,0,2:T(8,128)(2,1)}, s32[12]{0:T(128)S(1)}, s32[]{:T(128)}, /*index=5*/bf...) while((s32[]{:T(128)}, f32[384,2,128]{0,2,1:T(8,128)S(1)}, ...), condition=%wide.region_6.7_spmd.clone, body=%wide.region_5.6_spmd.clone.sunk | while | flops 305234816 | bytes 5911735 | solution.py:36
  583.3 90.7 %reduce-scatter.9.cloned.1.call-done = bf16[16,128]{1,0:T(8,128)(2,1)} async-done(((bf16[256,128]{1,0:T(8,128)(2,1)}), bf16[16,128]{1,0:T(8,128)(2,1)}) %reduce-scatter.9.cloned.1.call-update) | async-done | bytes 4112
  (503 shorter events, 183.4 us)
Async XLA Ops:
  7.2 87.3 %all-gather.5.cloned.1.call-start = ((), (), s32[]{:S(2)}) async-start(), calls=%async_computation.2 | async-start | bytes 1671168 | tf_op jit(solution)/shard_map/all_gather | solution.py:212
  8.3 5.4 copy-start.11
  11.0 3.5 copy-start.10
  11.0 4.3 copy-start.8
  11.8 164.2 %all-gather.7.cloned.1.call-start = ((), (), s32[]{:S(2)}) async-start(), calls=%async_computation.3 | async-start | bytes 1671168 | tf_op jit(solution)/shard_map/all_gather | solution.py:213
  14.5 329.1 %all-gather.9.cloned.1.call-start = ((), (), s32[]{:S(2)}) async-start(), calls=%async_computation.4 | async-start | bytes 3342336 | tf_op jit(solution)/shard_map/all_gather | solution.py:269
  15.3 354.3 %all-gather.11.cloned.1.call-start = ((), (), s32[]{:S(2)}) async-start(), calls=%async_computation.5 | async-start | bytes 3342336 | tf_op jit(solution)/shard_map/all_gather | solution.py:270
  16.1 505.6 %reduce-scatter.7.cloned.1.call-start = ((), (), s32[]{:S(2)}) async-start(), calls=%async_computation.6 | async-start | bytes 1114112
  369.6 84.4 %copy-start.12 = (s32[384,16]{0,1:T(8,128)S(1)}, s32[384,16]{0,1:T(8,128)}, u32[]{:S(2)}) copy-start(s32[384,16]{0,1:T(8,128)} %copy-done.11) | copy-start | bytes 73732
  373.3 1.7 copy-start.2
  380.4 1.7 copy-start.2
  387.4 1.7 copy-start.2
  394.4 1.7 copy-start.2
  401.4 1.7 copy-start.2
  408.5 1.7 copy-start.2
  422.5 1.7 copy-start.2
  429.5 1.7 copy-start.2
  436.6 1.7 copy-start.2
  443.6 1.7 copy-start.2
  450.6 1.7 copy-start.2
  453.9 2.8 copy-start.4
  460.5 64.7 %copy-start.1 = (bf16[384,2,128]{2,0,1:T(8,128)(2,1)S(1)}, bf16[384,2,128]{2,0,1:T(8,128)(2,1)}, u32[]{:S(2)}) copy-start(bf16[384,2,128]{2,0,1:T(8,128)(2,1)} %get-tuple-element.743) | copy-start | bytes 589828
  460.5 64.7 %copy-start.9 = (bf16[384,2,128]{2,0,1:T(8,128)(2,1)S(1)}, bf16[384,2,128]{2,0,1:T(8,128)(2,1)}, u32[]{:S(2)}) copy-start(bf16[384,2,128]{2,0,1:T(8,128)(2,1)} %copy.68) | copy-start | bytes 589828
  460.5 213.4 %reduce-scatter.9.cloned.1.call-start = ((), (), s32[]{:S(2)}) async-start(), calls=%async_computation.7 | async-start | bytes 69632
  (28 other events, 42.3 us)
Sparse Core Ops, SparseCore 0:
  11.9 82.4 all-gather.4
  97.1 78.8 all-gather.6
  179.2 95.3 all-gather.8
  277.1 92.4 all-gather.10
  460.6 60.9 reduce-scatter.6
  525.5 148.3 reduce-scatter.8
where the time goes:
time: 690 us; the launch traced here: 682 us
  waiting for transfers between devices  338 us (49%)
  matrix products  104 us (15%)
  blocking collectives  95.3 us (14%)
  local copies, waits for them, and re-layouts  91.7 us (13%)
  loops' own time  26.6 us (4%)
  between operations  14.4 us (2%)
  other arithmetic  12.5 us (2%)
    unnamed x8, waiting for transfers between devices  152 us
    all_gather x1, waiting for transfers between devices, per_device(): lax.all_gather(own_values, 'ctx', axis=0, tiled=True)  81.5 us
    all_gather x1, waiting for transfers between devices, per_device(): lax.all_gather(own_keys, 'ctx', axis=0, tiled=True)  78.3 us
    all_gather x1, blocking collectives, per_device(): lax.all_gather(fix_heads.T, 'ctx', axis=0, tiled=True)  64.6 us
    dynamic_slice x84, local copies, waits for them, and re-layouts, over_blocks(): lax.scan(advance, carried, (jnp.arange(block_count, dtype=jnp.int32), sha...  46 us
    all_gather x1, blocking collectives, per_device(): lax.all_gather(log_heads.T, 'ctx', axis=0, tiled=True)  30.7 us
    another operation x3, loops' own time, over_blocks(): lax.scan(advance, carried, (jnp.arange(block_count, dtype=jnp.int32), sha...  26.6 us
    all_gather x1, waiting for transfers between devices, per_device(): lax.all_gather(grad_out, 'ctx', axis=0, tiled=True)  26 us
  transfers between devices with their start and end apart: 6, of which 5 were waited for; matrix products, arithmetic and copies ran while one was open for 17% of the time, Pallas kernels for 0%

commit v1 on v0

v1 whole, which is shorter than its diff:
```python
import functools
import jax
import jax.numpy as jnp
from jax import lax
from jax.experimental import pallas as pl
from jax.experimental.pallas import tpu as pltpu
from jax.sharding import PartitionSpec as P

KVH = 8
HD = 128
SUB = 16
CODES = 256
GROUP = 4
COLS = HD // SUB
HEADS = 2
TILE = 256
LANES = 128
NEGATIVE = -1e30
SCALE = HD ** -0.5
LOG2E = 1.4426950408889634
F32 = jnp.float32
BF = jnp.bfloat16


def nn(a, b):
    return lax.dot_general(a, b, (((1,), (0,)), ((), ())), preferred_element_type=F32)


def nt(a, b):
    return lax.dot_general(a, b, (((1,), (1,)), ((), ())), preferred_element_type=F32)


def kernel(meta, q_ref, g_ref, codes_ref, bk_ref, bv_ref, attn_ref, qg_ref, book_ref,
           s_ref, kt_ref, vt_ref, tk_ref, tv_ref, m_ref, l_ref, c_ref, o_ref, dq_ref, acc_ref,
           qt_ref, gt_ref, x_ref):
    rows = q_ref.shape[0]
    own_first = meta[0]
    kv = meta[1]
    n_full = own_first // TILE
    n_all = (own_first + rows // HEADS + TILE - 1) // TILE
    tk_ref[...] = bk_ref[kv].astype(F32).T
    tv_ref[...] = bv_ref[kv].astype(F32).T
    qt_ref[...] = q_ref[...].astype(F32).T.astype(BF)
    gt_ref[...] = g_ref[...].astype(F32).T.astype(BF)
    m_ref[...] = jnp.full((rows, LANES), NEGATIVE, F32)
    l_ref[...] = jnp.zeros((rows, LANES), F32)
    o_ref[...] = jnp.zeros((rows, HD), F32)
    dq_ref[...] = jnp.zeros((rows, HD), F32)
    acc_ref[...] = jnp.zeros(acc_ref.shape, F32)
    x_ref[...] = jnp.zeros(x_ref.shape, BF)

    def decode(j):
        for half in range(2):
            codes = codes_ref[2 * j + half]
            for s in range(SUB):
                idx = jnp.broadcast_to(codes[s:s + 1], (COLS, LANES))
                low = idx & (LANES - 1)
                upper = idx >= LANES
                r = slice(s * COLS, (s + 1) * COLS)
                for t_ref, out in ((tk_ref, kt_ref), (tv_ref, vt_ref)):
                    a = jnp.take_along_axis(t_ref[r, :LANES], low, axis=1, mode="promise_in_bounds")
                    b = jnp.take_along_axis(t_ref[r, LANES:], low, axis=1, mode="promise_in_bounds")
                    out[j, r, half * LANES:(half + 1) * LANES] = jnp.where(upper, b, a).astype(BF)

    chunks = [slice(c, c + 256) for c in range(0, rows, 256)]

    def scores(j, masked):
        kt = kt_ref[j]
        for c in chunks:
            s = nn(q_ref[c], kt) * (SCALE * LOG2E)
            if masked:
                u = j * TILE + lax.broadcasted_iota(jnp.int32, s.shape, 1)
                t = own_first + (c.start + lax.broadcasted_iota(jnp.int32, s.shape, 0)) // HEADS
                s = jnp.where(u <= t, s, NEGATIVE)
            s_ref[j, c] = s
            m_ref[c] = jnp.maximum(m_ref[c], jnp.maximum(s[:, :LANES], s[:, LANES:]))

    def step_a(j, masked):
        decode(j)
        scores(j, masked)

    lax.fori_loop(0, n_full, lambda j, _: (step_a(j, False), 0)[1], 0)
    lax.fori_loop(n_full, n_all, lambda j, _: (step_a(j, True), 0)[1], 0)
    for c in chunks:
        m_ref[c] = jnp.broadcast_to(jnp.max(m_ref[c], axis=1, keepdims=True), (256, LANES))

    def step_b(j, _):
        vt = vt_ref[j]
        for c in chunks:
            m = m_ref[c]
            s = s_ref[j, c]
            e0 = jnp.exp2(s[:, :LANES] - m)
            e1 = jnp.exp2(s[:, LANES:] - m)
            l_ref[c] = l_ref[c] + (e0 + e1)
            e = jnp.concatenate([e0, e1], axis=1).astype(BF)
            o_ref[c] += nt(e, vt)
        return 0

    lax.fori_loop(0, n_all, step_b, 0)
    for c in chunks:
        total = jnp.sum(l_ref[c], axis=1, keepdims=True)
        out = (o_ref[c] / total).astype(BF)
        attn_ref[c] = out
        fix = jnp.sum(g_ref[c].astype(F32) * out.astype(F32), axis=1, keepdims=True)
        c_ref[c] = jnp.broadcast_to(fix, (256, LANES))
        m_ref[c] = m_ref[c] + jnp.log2(total)

    hi_iota = lax.broadcasted_iota(jnp.int32, (64, TILE), 0).astype(F32).astype(BF)
    one, zero = jnp.ones((64, TILE), BF), jnp.zeros((64, TILE), BF)
    zx = jnp.zeros((2 * COLS, TILE), BF)

    def code_sums(j):
        codes = jnp.concatenate([codes_ref[2 * j], codes_ref[2 * j + 1]], axis=1)
        high = (((codes >> 2) & 3) * 16 + (codes >> 4)).astype(F32).astype(BF)
        low = (codes & 3).astype(F32).astype(BF)
        for grp in range(4):
            his, xs = [], []
            for s in range(4 * grp, 4 * grp + 4):
                his.append(jnp.where(hi_iota == jnp.broadcast_to(high[s:s + 1], (64, TILE)), one, zero))
                x = x_ref[s * 16:(s + 1) * 16]
                lo = jnp.broadcast_to(low[s:s + 1], (16, TILE))
                for v in range(4):
                    xs.append(jnp.where(lo == jnp.full((16, TILE), v, BF), x, zx))
            acc_ref[grp] += nt(jnp.concatenate(his, axis=0), jnp.concatenate(xs, axis=0))

    def step_c(j, _):
        code_sums(jnp.maximum(j - 1, 0))
        vt, kt = vt_ref[j], kt_ref[j]
        dv = jnp.zeros((HD, TILE), F32)
        dk = jnp.zeros((HD, TILE), F32)
        for c in chunks:
            lse, fix = m_ref[c], c_ref[c]
            s = s_ref[j, c]
            w = jnp.exp2(s - jnp.concatenate([lse, lse], axis=1))
            dp = nn(g_ref[c], vt)
            ds = (w * (dp - jnp.concatenate([fix, fix], axis=1))).astype(BF)
            dq_ref[c] += nt(ds, kt)
            dv += nn(gt_ref[:, c], w.astype(BF))
            dk += nn(qt_ref[:, c], ds)
        dk = dk * SCALE
        for s in range(SUB):
            r = slice(s * COLS, (s + 1) * COLS)
            x_ref[s * 16:(s + 1) * 16] = jnp.concatenate([dk[r], dv[r]], axis=0).astype(BF)
        return 0

    lax.fori_loop(0, n_all, step_c, 0)
    code_sums(n_all - 1)
    qg_ref[...] = (dq_ref[...] * SCALE).astype(BF)
    for s in range(SUB):
        a = acc_ref[s // 4, (s % 4) * 64:(s % 4 + 1) * 64, (s % 4) * 64:(s % 4 + 1) * 64].astype(BF)
        for q in range(4):
            book_ref[s * 16:(s + 1) * 16, q * 64:(q + 1) * 64] = a[q * 16:(q + 1) * 16]


def attend(meta, q, g, codes, bk, bv):
    rows = q.shape[0]
    tiles = codes.shape[0] // 2
    vm = pl.BlockSpec(memory_space=pltpu.VMEM)
    return pl.pallas_call(
        kernel,
        out_shape=(jax.ShapeDtypeStruct((rows, HD), BF), jax.ShapeDtypeStruct((rows, HD), BF),
                   jax.ShapeDtypeStruct((CODES, 2 * HD), BF)),
        in_specs=[pl.BlockSpec(memory_space=pltpu.SMEM)] + [vm] * 5,
        out_specs=[vm] * 3,
        scratch_shapes=[
            pltpu.VMEM((tiles, rows, TILE), F32),
            pltpu.VMEM((tiles, HD, TILE), BF),
            pltpu.VMEM((tiles, HD, TILE), BF),
            pltpu.VMEM((HD, CODES), F32),
            pltpu.VMEM((HD, CODES), F32),
            pltpu.VMEM((rows, LANES), F32),
            pltpu.VMEM((rows, LANES), F32),
            pltpu.VMEM((rows, LANES), F32),
            pltpu.VMEM((rows, HD), F32),
            pltpu.VMEM((rows, HD), F32),
            pltpu.VMEM((4, 256, 256), F32),
            pltpu.VMEM((HD, rows), BF),
            pltpu.VMEM((HD, rows), BF),
            pltpu.VMEM((CODES, TILE), BF),
        ],
        compiler_params=pltpu.CompilerParams(vmem_limit_bytes=48 * 1024 * 1024),
    )(meta, q, g, codes, bk, bv)


def per_device(queries, codes, codebook_k, codebook_v, grad_out):
    row_count, head_count, columns = queries.shape
    n_ctx, n_head = lax.axis_size("ctx"), lax.axis_size("head")
    kv = lax.axis_index("head") * head_count // GROUP
    own_first = lax.axis_index("ctx") * row_count
    own_codes = lax.dynamic_slice_in_dim(codes, kv * SUB, SUB, 1)
    own_codes = own_codes.reshape(row_count // LANES, LANES, SUB).transpose(0, 2, 1)
    spread = jnp.broadcast_to(own_codes[None], (n_ctx,) + own_codes.shape)
    all_codes = lax.all_to_all(spread, "ctx", 0, 0).reshape(-1, SUB, LANES)
    meta = jnp.stack([own_first, kv]).astype(jnp.int32)
    attention, query_grad, books = attend(
        meta,
        queries.reshape(-1, columns),
        grad_out.reshape(-1, columns),
        all_codes,
        codebook_k,
        codebook_v,
    )
    parts = lax.all_to_all(books, ("head", "ctx"), 0, 0, tiled=True)
    sums = jnp.sum(parts.astype(F32).reshape(KVH, -1, parts.shape[1]), axis=1)
    sums = sums.reshape(KVH, CODES // n_ctx, 2, columns // n_head)
    return (
        attention.reshape(queries.shape),
        query_grad.reshape(queries.shape),
        sums[:, :, 0],
        sums[:, :, 1],
    )


def solution(mesh):
    placed = (P("ctx", "head", None), P("ctx", None), P(), P(), P("ctx", "head", None))
    return jax.shard_map(
        per_device,
        mesh=mesh,
        in_specs=placed,
        out_specs=(
            P("ctx", "head", None),
            P("ctx", "head", None),
            P(None, "ctx", "head"),
            P(None, "ctx", "head"),
        ),
        check_vma=False,
    )
```

time: 690 us -> 91.1 us (0.13); the launches traced: 682 us -> 90.9 us
  waiting for transfers between devices: 338 us -> 12.1 us
  matrix products: 104 us -> 0 us
  local copies, waits for them, and re-layouts: 91.7 us -> 4.26 us
  blocking collectives: 95.3 us -> 55.8 us
  loops' own time: 26.6 us -> 0 us
  between operations: 14.4 us -> 0.78 us
  other arithmetic: 12.5 us -> 0.78 us
  starting transfers between devices: 0.25 us -> 11.6 us
    all_gather x4 -> x0, waiting for transfers between devices: 186 us -> none  [the longest x1 81.5 us: per_device(): lax.all_gather(own_values, 'ctx', axis=0, tiled=True)]
    unnamed x8 -> x0, waiting for transfers between devices: 152 us -> none
    dot_general x88 -> x0, matrix products: 104 us -> none  [the longest x12 19.9 us: key_grad_step(): jnp.einsum('auk,uaf->kaf', linear_bias_slopes, query_subspace_slice, pref...]
    all_gather x2 -> x0, blocking collectives: 95.3 us -> none  [the longest x1 64.6 us: per_device(): lax.all_gather(fix_heads.T, 'ctx', axis=0, tiled=True)]
    all_to_all x0 -> x1, blocking collectives: none -> 55.8 us  [per_device(): parts = lax.all_to_all(books, ('head', 'ctx'), 0, 0, tiled=True)]
    dynamic_slice x89 -> x1, local copies, waits for them, and re-layouts: 47.3 us -> 0.11 us  [per_device(): own_codes = lax.dynamic_slice_in_dim(codes, kv * SUB, SUB, 1)]
    another operation x3 -> x0, loops' own time: 26.6 us -> none  [over_blocks(): lax.scan(advance, carried, (jnp.arange(block_count, dtype=jnp.int32), sha...]
    squeeze x25 -> x0, local copies, waits for them, and re-layouts: 22.6 us -> none  [the longest x24 22 us: over_blocks(): lax.scan(advance, carried, (jnp.arange(block_count, dtype=jnp.int32), sha...]
  transfers between devices with their start and end apart: 6 -> 1, of which waited for: 5 -> 1; matrix products, arithmetic and copies ran while one was open for 17% -> 0% of each run, Pallas kernels for 0% -> 0%
where the time goes in v1:
time: 91.1 us; the launch traced here: 90.9 us
  blocking collectives  55.8 us (61%)
  waiting for transfers between devices  12.1 us (13%)
  starting transfers between devices  11.6 us (13%)
  Pallas kernels  5.52 us (6%)
  local copies, waits for them, and re-layouts  4.26 us (5%)
    all_to_all x1, blocking collectives, per_device(): parts = lax.all_to_all(books, ('head', 'ctx'), 0, 0, tiled=True)  55.8 us
    all_to_all x1, waiting for transfers between devices, per_device(): all_codes = lax.all_to_all(spread, 'ctx', 0, 0).reshape(-1, SUB, LANES)  12.1 us
    all_to_all x1, starting transfers between devices, per_device(): all_codes = lax.all_to_all(spread, 'ctx', 0, 0).reshape(-1, SUB, LANES)  11.6 us
    pallas_call x1, Pallas kernels, attend(): pl.pallas_call(kernel, out_shape=(jax.ShapeDtypeStruct((rows, HD), BF), j...  5.52 us
    unnamed x15, local copies, waits for them, and re-layouts  2.42 us
  transfers between devices with their start and end apart: 1, of which 1 were waited for; matrix products, arithmetic and copies ran while one was open for 0% of the time, Pallas kernels for 0%

profile of v1, /device:TPU:1, one launch (start us, length us, event | category | flops | bytes accessed | tf_op | source)
XLA Modules:
  0.0 90.9 jit_solution(15603748128410179431)
XLA Ops:
  0.6 0.0 copy-start
  0.7 0.9 copy-done
  1.6 0.1 constant_dynamic-slice_fusion
  1.7 0.0 copy-start.4
  1.7 0.1 copy.18
  1.8 0.0 copy-start.3
  1.8 0.0 copy-start.1
  1.8 0.0 copy-start.2
  1.8 0.8 broadcast_in_dim.2
  2.6 11.6 %all-to-all-start = ((s32[16,3,16,128]{3,2,1,0:T(8,128)}), s32[16,3,16,128]{3,2,1,0:T(8,128)S(1)}, u32[]{:S(2)}, u32[]{:S(2)}) async-start(s32[16,3,16,128]{3,2,1,0:T(8,128)} %broadcast_in_dim.2), calls=%async_computation | async-start | bytes 786432 | tf_op jit(solution)/shard_map/all_to_all | solution.py:193
  14.2 0.1 pad_add_fusion.meta
  14.3 12.1 %all-to-all-done = s32[16,3,16,128]{3,2,1,0:T(8,128)S(1)} async-done(((s32[16,3,16,128]{3,2,1,0:T(8,128)}), s32[16,3,16,128]{3,2,1,0:T(8,128)S(1)}, u32[]{:S(2)}, u32[]{:S(2)}) %all-to-all-start) | async-done | bytes 393248 | tf_op jit(solution)/shard_map/all_to_all | solution.py:193
  26.4 0.0 copy-done.4
  26.4 0.0 copy-done.3
  26.4 0.0 copy-done.1
  26.4 0.0 copy-done.2
  26.5 5.5 %shard_map.84 = (bf16[768,128]{1,0:T(8,128)(2,1)}, bf16[768,128]{1,0:T(8,128)(2,1)}, bf16[256,256]{1,0:T(8,128)(2,1)S(1)}) custom-call(s32[2]{0:T(128)S(1)} %pad_add_fusion.meta, bf16[768,128]{1,0:T(8,128)(2,1)S(1)} %bitcast.14, bf16[768,128]{1,0:T(8,128)(2,1)S(1)} %bitcast.15, s32[48,16,128]{2,1,0:T(8,128)S(1)} %bitcast.13, ...), custom_call_target="tpu_custom_call" | custom-call | tf_op jit(solution)/shard_map/pallas_call | solution.py:159
  32.0 0.5 broadcast.2
  32.5 0.7 reduce
  33.2 55.8 %all_to_all.14 = bf16[256,2,128]{2,1,0:T(2,128)(2,1)S(1)} all-to-all(bf16[256,2,128]{2,1,0:T(2,128)(2,1)S(1)} %reshape.44), channel_id=1, replica_groups=mesh['ctx'=16,'head'=16] {'head','ctx'}, dimensions={0} | all-to-all | bytes 262144 | tf_op jit(solution)/shard_map/all_to_all | solution.py:203
  89.1 0.2 reshape.42
  89.3 0.1 fusion
  89.5 0.7 copy.16
  90.2 0.7 copy.17
  (5 shorter events, 0.1 us)
Async XLA Ops:
  0.6 0.9 %copy-start = (s32[384,128]{1,0:T(8,128)S(1)}, s32[384,128]{1,0:T(8,128)}, u32[]{:S(2)}) copy-start(s32[384,128]{1,0:T(8,128)} %param.6) | copy-start | bytes 589828
  1.7 24.8 %copy-start.4 = (bf16[384,2,128]{2,1,0:T(2,128)(2,1)S(1)}, bf16[384,2,128]{2,1,0:T(2,128)(2,1)}, u32[]{:S(2)}) copy-start(bf16[384,2,128]{2,1,0:T(2,128)(2,1)} %param.9) | copy-start | bytes 589828
  1.8 24.6 %copy-start.3 = (bf16[384,2,128]{2,1,0:T(2,128)(2,1)S(1)}, bf16[384,2,128]{2,1,0:T(2,128)(2,1)}, u32[]{:S(2)}) copy-start(bf16[384,2,128]{2,1,0:T(2,128)(2,1)} %param.5) | copy-start | bytes 589828
  1.8 24.6 %copy-start.1 = (bf16[8,256,128]{2,1,0:T(8,128)(2,1)S(1)}, bf16[8,256,128]{2,1,0:T(8,128)(2,1)}, u32[]{:S(2)}) copy-start(bf16[8,256,128]{2,1,0:T(8,128)(2,1)} %bk_ref.1) | copy-start | bytes 1572868
  1.8 24.6 %copy-start.2 = (bf16[8,256,128]{2,1,0:T(8,128)(2,1)S(1)}, bf16[8,256,128]{2,1,0:T(8,128)(2,1)}, u32[]{:S(2)}) copy-start(bf16[8,256,128]{2,1,0:T(8,128)(2,1)} %bv_ref.1) | copy-start | bytes 1572868
  2.6 23.8 %all-to-all-start = ((s32[16,3,16,128]{3,2,1,0:T(8,128)}), s32[16,3,16,128]{3,2,1,0:T(8,128)S(1)}, u32[]{:S(2)}, u32[]{:S(2)}) async-start(s32[16,3,16,128]{3,2,1,0:T(8,128)} %broadcast_in_dim.2), calls=%async_computation | async-start | bytes 786432 | tf_op jit(solution)/shard_map/all_to_all | solution.py:193

commit v2 on v1

v2 whole, which is shorter than its diff:
```python
import functools
import jax
import jax.numpy as jnp
from jax import lax
from jax.experimental import pallas as pl
from jax.experimental.pallas import tpu as pltpu
from jax.sharding import PartitionSpec as P

KVH = 8
HD = 128
SUB = 16
CODES = 256
GROUP = 4
COLS = HD // SUB
HEADS = 2
TILE = 512
PARTS = 3
WIDE = PARTS * TILE
CHUNK = 384
LANES = 128
NEGATIVE = -1e30
SCALE = HD ** -0.5
LOG2E = 1.4426950408889634
F32 = jnp.float32
BF = jnp.bfloat16


def nn(a, b):
    return lax.dot_general(a, b, (((1,), (0,)), ((), ())), preferred_element_type=F32)


def nt(a, b):
    return lax.dot_general(a, b, (((1,), (1,)), ((), ())), preferred_element_type=F32)


def kernel(meta, q_ref, g_ref, codes_ref, bk_ref, bv_ref, attn_ref, qg_ref, book_ref,
           s_ref, kt_ref, vt_ref, next_ref, tk_ref, tv_ref, m_ref, l_ref, c_ref, o_ref, dq_ref, acc_ref,
           qt_ref, gt_ref, *bufs):
    rows = q_ref.shape[0]
    own_first = meta[0]
    kv = meta[1]
    n_all = (own_first + rows // HEADS + WIDE - 1) // WIDE
    last = n_all - 1
    w_refs, d_refs, x_refs = bufs[:PARTS], bufs[PARTS:2 * PARTS], bufs[2 * PARTS:]
    tk_ref[...] = bk_ref[kv].astype(F32).T
    tv_ref[...] = bv_ref[kv].astype(F32).T
    qt_ref[...] = q_ref[...].astype(F32).T.astype(BF)
    gt_ref[...] = g_ref[...].astype(F32).T.astype(BF)
    m_ref[...] = jnp.full((rows, LANES), NEGATIVE, F32)
    l_ref[...] = jnp.zeros((rows, LANES), F32)
    o_ref[...] = jnp.zeros((rows, HD), F32)
    dq_ref[...] = jnp.zeros((rows, HD), F32)
    acc_ref[...] = jnp.zeros(acc_ref.shape, F32)
    for ref in (w_refs[-1], d_refs[-1], *x_refs[-2:]):
        ref[...] = jnp.zeros(ref.shape, BF)

    def decode(j, t_ref, out):
        for part in range(WIDE // LANES):
            codes = codes_ref[j * (WIDE // LANES) + part]
            for s in range(SUB):
                idx = jnp.broadcast_to(codes[s:s + 1], (COLS, LANES))
                low = idx & (LANES - 1)
                upper = idx >= LANES
                r = slice(s * COLS, (s + 1) * COLS)
                a = jnp.take_along_axis(t_ref[r, :LANES], low, axis=1, mode="promise_in_bounds")
                b = jnp.take_along_axis(t_ref[r, LANES:], low, axis=1, mode="promise_in_bounds")
                out[r, part * LANES:(part + 1) * LANES] = jnp.where(upper, b, a).astype(BF)

    chunks = [slice(c, c + CHUNK) for c in range(0, rows, CHUNK)]
    parts = [slice(p * TILE, (p + 1) * TILE) for p in range(PARTS)]

    def scores(j, masked):
        for c in chunks:
            top = m_ref[c]
            for p in parts:
                s = nn(q_ref[c], kt_ref[j, :, p]) * (SCALE * LOG2E)
                if masked:
                    u = j * WIDE + p.start + lax.broadcasted_iota(jnp.int32, s.shape, 1)
                    t = own_first + (c.start + lax.broadcasted_iota(jnp.int32, s.shape, 0)) // HEADS
                    s = jnp.where(u <= t, s, NEGATIVE)
                s_ref[j, c, p] = s
                for lane in range(0, TILE, LANES):
                    top = jnp.maximum(top, s[:, lane:lane + LANES])
            m_ref[c] = top

    def step_a(j, _):
        scores(j, False)
        decode(j + 1, tk_ref, next_ref)
        kt_ref[j + 1] = next_ref[...]
        return 0

    decode(0, tk_ref, next_ref)
    kt_ref[0] = next_ref[...]
    lax.fori_loop(0, last, step_a, 0)
    scores(last, True)
    decode(0, tv_ref, next_ref)
    vt_ref[0] = next_ref[...]
    for c in chunks:
        m_ref[c] = jnp.broadcast_to(jnp.max(m_ref[c], axis=1, keepdims=True), (CHUNK, LANES))

    def step_b(j, more):
        for c in chunks:
            m = m_ref[c]
            total = l_ref[c]
            es = []
            for p in range(0, WIDE, LANES):
                e = jnp.exp2(s_ref[j, c, p:p + LANES] - m)
                total = total + e
                es.append(e)
            l_ref[c] = total
            o_ref[c] += nt(jnp.concatenate(es, axis=1).astype(BF), vt_ref[j])
        if more:
            decode(j + 1, tv_ref, next_ref)
            vt_ref[j + 1] = next_ref[...]
        return 0

    lax.fori_loop(0, last, lambda j, _: step_b(j, True), 0)
    step_b(last, False)
    for c in chunks:
        total = jnp.sum(l_ref[c], axis=1, keepdims=True)
        out = (o_ref[c] / total).astype(BF)
        attn_ref[c] = out
        fix = jnp.sum(g_ref[c].astype(F32) * out.astype(F32), axis=1, keepdims=True)
        c_ref[c] = jnp.broadcast_to(fix, (CHUNK, LANES))
        m_ref[c] = m_ref[c] + jnp.log2(total)

    hi_iota = lax.broadcasted_iota(jnp.int32, (64, TILE), 0).astype(F32).astype(BF)
    one, zero = jnp.ones((64, TILE), BF), jnp.zeros((64, TILE), BF)
    zx = jnp.zeros((2 * COLS, TILE), BF)

    def code_sums(j, p):
        base = (j * WIDE + p * TILE) // LANES
        codes = jnp.concatenate([codes_ref[base + i] for i in range(TILE // LANES)], axis=1)
        high = (((codes >> 2) & 1) * 32 + (codes >> 4) * 2 + ((codes >> 3) & 1)).astype(F32).astype(BF)
        low = (codes & 3).astype(F32).astype(BF)
        for grp in range(4):
            his, xs = [], []
            for s in range(4 * grp, 4 * grp + 4):
                his.append(jnp.where(hi_iota == jnp.broadcast_to(high[s:s + 1], (64, TILE)), one, zero))
                x = x_refs[p][s * 16:(s + 1) * 16]
                lo = jnp.broadcast_to(low[s:s + 1], (16, TILE))
                for v in range(4):
                    xs.append(jnp.where(lo == jnp.full((16, TILE), v, BF), x, zx))
            acc_ref[grp] += nt(jnp.concatenate(his, axis=0), jnp.concatenate(xs, axis=0))

    def slopes(j, p):
        for c in chunks:
            lse, fix = m_ref[c], c_ref[c]
            w = jnp.exp2(s_ref[j, c, parts[p]] - jnp.concatenate([lse] * (TILE // LANES), axis=1))
            dp = nn(g_ref[c], vt_ref[j, :, parts[p]])
            w_refs[p][c] = w.astype(BF)
            d_refs[p][c] = (w * (dp - jnp.concatenate([fix] * (TILE // LANES), axis=1))).astype(BF)

    def products(j, p):
        for c in chunks:
            dq_ref[c] += nt(d_refs[p][c], kt_ref[j, :, parts[p]])
        dv = nn(gt_ref[...], w_refs[p][...])
        dk = nn(qt_ref[...], d_refs[p][...]) * SCALE
        for s in range(SUB):
            r = slice(s * COLS, (s + 1) * COLS)
            x_refs[p][s * 16:(s + 1) * 16] = jnp.concatenate([dk[r], dv[r]], axis=0).astype(BF)

    def step_c(j, _):
        before = jnp.maximum(j - 1, 0)
        for p in range(PARTS):
            code_sums(before if p < 2 else j, (p - 2) % PARTS)
            products(before if p < 1 else j, (p - 1) % PARTS)
            slopes(j, p)
        return 0

    lax.fori_loop(0, n_all, step_c, 0)
    products(last, PARTS - 1)
    code_sums(last, PARTS - 2)
    code_sums(last, PARTS - 1)
    qg_ref[...] = (dq_ref[...] * SCALE).astype(BF)
    for s in range(SUB):
        at = s % 4 * 64
        a = acc_ref[s // 4, at:at + 64, at:at + 64].astype(BF)
        book_ref[s * 32:(s + 1) * 32] = jnp.concatenate([a[:32], a[32:]], axis=1)


def attend(meta, q, g, codes, bk, bv):
    rows = q.shape[0]
    tiles = codes.shape[0] * LANES // WIDE
    vm = pl.BlockSpec(memory_space=pltpu.VMEM)
    return pl.pallas_call(
        kernel,
        out_shape=(jax.ShapeDtypeStruct((rows, HD), BF), jax.ShapeDtypeStruct((rows, HD), BF),
                   jax.ShapeDtypeStruct((2 * CODES, HD), BF)),
        in_specs=[pl.BlockSpec(memory_space=pltpu.SMEM)] + [vm] * 5,
        out_specs=[vm] * 3,
        scratch_shapes=[
            pltpu.VMEM((tiles, rows, WIDE), F32),
            pltpu.VMEM((tiles, HD, WIDE), BF),
            pltpu.VMEM((tiles, HD, WIDE), BF),
            pltpu.VMEM((HD, WIDE), BF),
            pltpu.VMEM((HD, CODES), F32),
            pltpu.VMEM((HD, CODES), F32),
            pltpu.VMEM((rows, LANES), F32),
            pltpu.VMEM((rows, LANES), F32),
            pltpu.VMEM((rows, LANES), F32),
            pltpu.VMEM((rows, HD), F32),
            pltpu.VMEM((rows, HD), F32),
            pltpu.VMEM((4, 256, 256), F32),
            pltpu.VMEM((HD, rows), BF),
            pltpu.VMEM((HD, rows), BF),
        ]
        + [pltpu.VMEM((rows, TILE), BF)] * (2 * PARTS)
        + [pltpu.VMEM((CODES, TILE), BF)] * PARTS,
        compiler_params=pltpu.CompilerParams(vmem_limit_bytes=48 * 1024 * 1024),
    )(meta, q, g, codes, bk, bv)


def gather_sums(parts_ref, k_ref, v_ref):
    n = parts_ref.shape[0]
    pair = n // KVH
    row = lax.broadcasted_iota(jnp.int32, (KVH, n), 1)
    head = lax.broadcasted_iota(jnp.int32, (KVH, n), 0)
    src = lax.broadcasted_iota(jnp.int32, (HD, HD), 0)
    dst = lax.broadcasted_iota(jnp.int32, (HD, HD), 1)
    parts = parts_ref[...]
    halves = []
    for k in range(2):
        pick = ((row // pair == head) & (row % 2 == k)).astype(F32).astype(BF)
        halves.append(nn(pick, parts))
    for side, out in enumerate((k_ref, v_ref)):
        total = jnp.zeros((KVH, HD), F32)
        for k in range(2):
            want = src % 8 * 16 + 8 * k + src // 16
            place = ((dst == want) & (src // 8 % 2 == side)).astype(F32)
            total += lax.dot_general(halves[k], place, (((1,), (0,)), ((), ())), precision=lax.Precision.HIGHEST, preferred_element_type=F32)
        for j in range(COLS):
            out[:, j, :] = total[:, j * 16:(j + 1) * 16]


def finish(parts):
    vm = pl.BlockSpec(memory_space=pltpu.VMEM)
    shape = jax.ShapeDtypeStruct((KVH, COLS, 16), F32)
    return pl.pallas_call(gather_sums, out_shape=(shape, shape), in_specs=[vm], out_specs=(vm, vm))(parts)


def per_device(queries, codes, codebook_k, codebook_v, grad_out):
    row_count, head_count, columns = queries.shape
    n_ctx, n_head = lax.axis_size("ctx"), lax.axis_size("head")
    kv = lax.axis_index("head") * head_count // GROUP
    own_first = lax.axis_index("ctx") * row_count
    own_codes = lax.dynamic_slice_in_dim(codes, kv * SUB, SUB, 1)
    own_codes = own_codes.reshape(row_count // LANES, LANES, SUB).transpose(0, 2, 1)
    own_codes = own_codes.reshape(-1, LANES).astype(BF)
    spread = jnp.broadcast_to(own_codes[None], (n_ctx,) + own_codes.shape)
    all_codes = lax.all_to_all(spread, "ctx", 0, 0, tiled=True).astype(jnp.int32).reshape(-1, SUB, LANES)
    meta = jnp.stack([own_first, kv]).astype(jnp.int32)
    attention, query_grad, books = attend(
        meta,
        queries.reshape(-1, columns),
        grad_out.reshape(-1, columns),
        all_codes,
        codebook_k,
        codebook_v,
    )
    parts = lax.all_to_all(books.reshape(CODES, 2, columns), ("head", "ctx"), 0, 0, tiled=True)
    sums_k, sums_v = finish(parts.reshape(books.shape))
    return (
        attention.reshape(queries.shape),
        query_grad.reshape(queries.shape),
        sums_k.transpose(0, 2, 1),
        sums_v.transpose(0, 2, 1),
    )


def solution(mesh):
    placed = (P("ctx", "head", None), P("ctx", None), P(), P(), P("ctx", "head", None))
    return jax.shard_map(
        per_device,
        mesh=mesh,
        in_specs=placed,
        out_specs=(
            P("ctx", "head", None),
            P("ctx", "head", None),
            P(None, "ctx", "head"),
            P(None, "ctx", "head"),
        ),
        check_vma=False,
    )
```

time: 91.1 us -> 72.5 us (0.80)
  blocking collectives: 55.8 us -> 38.2 us
  Pallas kernels: 5.52 us -> 10.6 us
  waiting for transfers between devices: 12.1 us -> 8.95 us
  local copies, waits for them, and re-layouts: 4.26 us -> 1.85 us
    all_to_all x1, blocking collectives: 55.8 us -> 38.2 us  [per_device(): lax.all_to_all(books.reshape(CODES, 2, columns), ('head', 'ctx'), 0, 0, t...]
    all_to_all x1, waiting for transfers between devices: 12.1 us -> 8.95 us  [per_device(): lax.all_to_all(spread, 'ctx', 0, 0, tiled=True).astype(jnp.int32)]
    pallas_call x1, Pallas kernels: 5.52 us -> 8.46 us  [attend(): pl.pallas_call(kernel, out_shape=(jax.ShapeDtypeStruct((rows, HD), BF), j...]
    pallas_call x0 -> x1, Pallas kernels: none -> 2.15 us  [finish(): pl.pallas_call(gather_sums, out_shape=(shape, shape), in_specs=[vm], out_...]
    unnamed x15 -> x11, local copies, waits for them, and re-layouts: 2.42 us -> 1.02 us
where the time goes in v2:
time: 72.5 us; the launch traced here: 72.2 us
  blocking collectives  38.2 us (53%)
  starting transfers between devices  11.7 us (16%)
  Pallas kernels  10.6 us (15%)
  waiting for transfers between devices  8.95 us (12%)
  local copies, waits for them, and re-layouts  1.85 us (3%)
  between operations  0.76 us (1%)
    all_to_all x1, blocking collectives, per_device(): lax.all_to_all(books.reshape(CODES, 2, columns), ('head', 'ctx'), 0, 0, t...  38.2 us
    all_to_all x1, starting transfers between devices, per_device(): lax.all_to_all(spread, 'ctx', 0, 0, tiled=True).astype(jnp.int32)  11.7 us
    all_to_all x1, waiting for transfers between devices, per_device(): lax.all_to_all(spread, 'ctx', 0, 0, tiled=True).astype(jnp.int32)  8.95 us
    pallas_call x1, Pallas kernels, attend(): pl.pallas_call(kernel, out_shape=(jax.ShapeDtypeStruct((rows, HD), BF), j...  8.46 us
    pallas_call x1, Pallas kernels, finish(): pl.pallas_call(gather_sums, out_shape=(shape, shape), in_specs=[vm], out_...  2.15 us
  transfers between devices with their start and end apart: 1, of which 1 were waited for; matrix products, arithmetic and copies ran while one was open for 0% of the time, Pallas kernels for 0%

profile of v2, /device:TPU:1, one launch (start us, length us, event | category | flops | bytes accessed | tf_op | source)
XLA Modules:
  0.0 72.2 jit_solution(3453865667389860509)
XLA Ops:
  0.6 0.0 copy-start
  0.7 0.9 %copy-done = s32[384,128]{1,0:T(8,128)S(1)} copy-done((s32[384,128]{1,0:T(8,128)S(1)}, s32[384,128]{1,0:T(8,128)}, u32[]{:S(2)}) %copy-start) | copy-done | bytes 196632
  1.6 0.1 constant_dynamic-slice_fusion
  1.7 0.0 copy-start.4
  1.7 0.1 copy.13
  1.8 0.0 copy-start.3
  1.8 0.0 copy-start.2
  1.8 0.7 broadcast_in_dim.2
  2.6 0.0 copy-start.1
  2.6 11.7 %all-to-all-start = ((bf16[16,48,128]{2,1,0:T(8,128)(2,1)}), bf16[16,48,128]{2,1,0:T(8,128)(2,1)S(1)}, u32[]{:S(2)}, u32[]{:S(2)}) async-start(bf16[16,48,128]{2,1,0:T(8,128)(2,1)} %broadcast_in_dim.2), calls=%async_computation | async-start | bytes 393216 | tf_op jit(solution)/shard_map/all_to_all | solution.py:251
  14.3 0.1 pad_add_fusion.meta
  14.4 9.0 %all-to-all-done = bf16[16,48,128]{2,1,0:T(8,128)(2,1)S(1)} async-done(((bf16[16,48,128]{2,1,0:T(8,128)(2,1)}), bf16[16,48,128]{2,1,0:T(8,128)(2,1)S(1)}, u32[]{:S(2)}, u32[]{:S(2)}) %all-to-all-start) | async-done | bytes 196640 | tf_op jit(solution)/shard_map/all_to_all | solution.py:251
  23.4 0.0 copy-done.4
  23.4 0.0 copy-done.3
  23.4 0.0 copy-done.2
  23.4 0.0 copy-done.1
  23.4 8.5 %shard_map.84 = (bf16[768,128]{1,0:T(8,128)(2,1)}, bf16[768,128]{1,0:T(8,128)(2,1)}, bf16[512,128]{1,0:T(8,128)(2,1)S(1)}) custom-call(s32[2]{0:T(128)S(1)} %pad_add_fusion.meta, bf16[768,128]{1,0:T(8,128)(2,1)S(1)} %bitcast.16, bf16[768,128]{1,0:T(8,128)(2,1)S(1)} %bitcast.17, s32[48,16,128]{2,1,0:T(8,128)S(1)} %convert.1.codes_ref, ...), custom_call_target="tpu_custom_call" | custom-call | tf_op jit(solution)/shard_map/pallas_call | solution.py:186
  31.9 38.2 %all_to_all.10 = bf16[256,2,128]{2,1,0:T(2,128)(2,1)} all-to-all(bf16[256,2,128]{2,1,0:T(2,128)(2,1)S(1)} %bitcast.18), channel_id=1, replica_groups=mesh['ctx'=16,'head'=16] {'head','ctx'}, dimensions={0} | all-to-all | bytes 262144 | tf_op jit(solution)/shard_map/all_to_all | solution.py:261
  70.1 2.1 %shard_map.85 = (f32[8,8,16]{2,1,0:T(8,128)}, f32[8,8,16]{2,1,0:T(8,128)}) custom-call(bf16[512,128]{1,0:T(8,128)(2,1)} %bitcast.20), custom_call_target="tpu_custom_call" | custom-call | tf_op jit(solution)/shard_map/pallas_call | solution.py:239
  (4 shorter events, 0.1 us)
Async XLA Ops:
  0.6 0.9 %copy-start = (s32[384,128]{1,0:T(8,128)S(1)}, s32[384,128]{1,0:T(8,128)}, u32[]{:S(2)}) copy-start(s32[384,128]{1,0:T(8,128)} %param.6) | copy-start | bytes 589828
  1.7 21.7 %copy-start.4 = (bf16[384,2,128]{2,1,0:T(2,128)(2,1)S(1)}, bf16[384,2,128]{2,1,0:T(2,128)(2,1)}, u32[]{:S(2)}) copy-start(bf16[384,2,128]{2,1,0:T(2,128)(2,1)} %param.9) | copy-start | bytes 589828
  1.8 21.6 %copy-start.3 = (bf16[384,2,128]{2,1,0:T(2,128)(2,1)S(1)}, bf16[384,2,128]{2,1,0:T(2,128)(2,1)}, u32[]{:S(2)}) copy-start(bf16[384,2,128]{2,1,0:T(2,128)(2,1)} %param.5) | copy-start | bytes 589828
  1.8 21.5 %copy-start.2 = (bf16[8,256,128]{2,1,0:T(8,128)(2,1)S(1)}, bf16[8,256,128]{2,1,0:T(8,128)(2,1)}, u32[]{:S(2)}) copy-start(bf16[8,256,128]{2,1,0:T(8,128)(2,1)} %bv_ref.1) | copy-start | bytes 1572868
  2.6 20.8 %copy-start.1 = (bf16[8,256,128]{2,1,0:T(8,128)(2,1)S(1)}, bf16[8,256,128]{2,1,0:T(8,128)(2,1)}, u32[]{:S(2)}) copy-start(bf16[8,256,128]{2,1,0:T(8,128)(2,1)} %bk_ref.1) | copy-start | bytes 1572868
  2.6 20.8 %all-to-all-start = ((bf16[16,48,128]{2,1,0:T(8,128)(2,1)}), bf16[16,48,128]{2,1,0:T(8,128)(2,1)S(1)}, u32[]{:S(2)}, u32[]{:S(2)}) async-start(bf16[16,48,128]{2,1,0:T(8,128)(2,1)} %broadcast_in_dim.2), calls=%async_computation | async-start | bytes 393216 | tf_op jit(solution)/shard_map/all_to_all | solution.py:251

commit v3 on v2

--- a/solution.py
+++ b/solution.py
@@ -33,12 +33,12 @@
     return lax.dot_general(a, b, (((1,), (1,)), ((), ())), preferred_element_type=F32)
 
 
-def kernel(meta, q_ref, g_ref, codes_ref, bk_ref, bv_ref, attn_ref, qg_ref, book_ref,
+def kernel(q_ref, g_ref, codes_ref, bk_ref, bv_ref, attn_ref, qg_ref, book_ref,
            s_ref, kt_ref, vt_ref, next_ref, tk_ref, tv_ref, m_ref, l_ref, c_ref, o_ref, dq_ref, acc_ref,
            qt_ref, gt_ref, *bufs):
     rows = q_ref.shape[0]
-    own_first = meta[0]
-    kv = meta[1]
+    own_first = lax.axis_index("ctx") * (rows // HEADS)
+    kv = lax.axis_index("head") * HEADS // GROUP
     n_all = (own_first + rows // HEADS + WIDE - 1) // WIDE
     last = n_all - 1
     w_refs, d_refs, x_refs = bufs[:PARTS], bufs[PARTS:2 * PARTS], bufs[2 * PARTS:]
@@ -49,10 +49,6 @@
     m_ref[...] = jnp.full((rows, LANES), NEGATIVE, F32)
     l_ref[...] = jnp.zeros((rows, LANES), F32)
     o_ref[...] = jnp.zeros((rows, HD), F32)
-    dq_ref[...] = jnp.zeros((rows, HD), F32)
-    acc_ref[...] = jnp.zeros(acc_ref.shape, F32)
-    for ref in (w_refs[-1], d_refs[-1], *x_refs[-2:]):
-        ref[...] = jnp.zeros(ref.shape, BF)
 
     def decode(j, t_ref, out):
         for part in range(WIDE // LANES):
@@ -116,6 +112,10 @@
 
     lax.fori_loop(0, last, lambda j, _: step_b(j, True), 0)
     step_b(last, False)
+    dq_ref[...] = jnp.zeros((rows, HD), F32)
+    acc_ref[...] = jnp.zeros(acc_ref.shape, F32)
+    for ref in (w_refs[-1], d_refs[-1], *x_refs[-2:]):
+        ref[...] = jnp.zeros(ref.shape, BF)
     for c in chunks:
         total = jnp.sum(l_ref[c], axis=1, keepdims=True)
         out = (o_ref[c] / total).astype(BF)
@@ -179,7 +179,7 @@
         book_ref[s * 32:(s + 1) * 32] = jnp.concatenate([a[:32], a[32:]], axis=1)
 
 
-def attend(meta, q, g, codes, bk, bv):
+def attend(q, g, codes, bk, bv):
     rows = q.shape[0]
     tiles = codes.shape[0] * LANES // WIDE
     vm = pl.BlockSpec(memory_space=pltpu.VMEM)
@@ -187,7 +187,7 @@
         kernel,
         out_shape=(jax.ShapeDtypeStruct((rows, HD), BF), jax.ShapeDtypeStruct((rows, HD), BF),
                    jax.ShapeDtypeStruct((2 * CODES, HD), BF)),
-        in_specs=[pl.BlockSpec(memory_space=pltpu.SMEM)] + [vm] * 5,
+        in_specs=[vm] * 5,
         out_specs=[vm] * 3,
         scratch_shapes=[
             pltpu.VMEM((tiles, rows, WIDE), F32),
@@ -208,7 +208,7 @@
         + [pltpu.VMEM((rows, TILE), BF)] * (2 * PARTS)
         + [pltpu.VMEM((CODES, TILE), BF)] * PARTS,
         compiler_params=pltpu.CompilerParams(vmem_limit_bytes=48 * 1024 * 1024),
-    )(meta, q, g, codes, bk, bv)
+    )(q, g, codes, bk, bv)
 
 
 def gather_sums(parts_ref, k_ref, v_ref):
@@ -216,19 +216,16 @@
     pair = n // KVH
     row = lax.broadcasted_iota(jnp.int32, (KVH, n), 1)
     head = lax.broadcasted_iota(jnp.int32, (KVH, n), 0)
-    src = lax.broadcasted_iota(jnp.int32, (HD, HD), 0)
-    dst = lax.broadcasted_iota(jnp.int32, (HD, HD), 1)
-    parts = parts_ref[...]
-    halves = []
-    for k in range(2):
-        pick = ((row // pair == head) & (row % 2 == k)).astype(F32).astype(BF)
-        halves.append(nn(pick, parts))
+    src = lax.broadcasted_iota(jnp.int32, (HD, 4 * HD), 0)
+    dst = lax.broadcasted_iota(jnp.int32, (HD, 4 * HD), 1)
+    want = src // 8 % 2 * 256 + dst // 128 % 2 * 128 + src % 8 * 16 + dst // 128 % 2 * 8 + src // 16
+    placed = nn(parts_ref[...], (dst == want).astype(F32).astype(BF)).astype(BF)
     for side, out in enumerate((k_ref, v_ref)):
         total = jnp.zeros((KVH, HD), F32)
         for k in range(2):
-            want = src % 8 * 16 + 8 * k + src // 16
-            place = ((dst == want) & (src // 8 % 2 == side)).astype(F32)
-            total += lax.dot_general(halves[k], place, (((1,), (0,)), ((), ())), precision=lax.Precision.HIGHEST, preferred_element_type=F32)
+            pick = ((row // pair == head) & (row % 2 == k)).astype(F32).astype(BF)
+            at = (2 * side + k) * HD
+            total += nn(pick, placed[:, at:at + HD])
         for j in range(COLS):
             out[:, j, :] = total[:, j * 16:(j + 1) * 16]
 
@@ -236,22 +233,25 @@
 def finish(parts):
     vm = pl.BlockSpec(memory_space=pltpu.VMEM)
     shape = jax.ShapeDtypeStruct((KVH, COLS, 16), F32)
-    return pl.pallas_call(gather_sums, out_shape=(shape, shape), in_specs=[vm], out_specs=(vm, vm))(parts)
+    return pl.pallas_call(
+        gather_sums,
+        out_shape=(shape, shape),
+        in_specs=[vm],
+        out_specs=(vm, vm),
+        compiler_params=pltpu.CompilerParams(vmem_limit_bytes=4 * 1024 * 1024),
+    )(parts)
 
 
 def per_device(queries, codes, codebook_k, codebook_v, grad_out):
     row_count, head_count, columns = queries.shape
     n_ctx, n_head = lax.axis_size("ctx"), lax.axis_size("head")
     kv = lax.axis_index("head") * head_count // GROUP
-    own_first = lax.axis_index("ctx") * row_count
     own_codes = lax.dynamic_slice_in_dim(codes, kv * SUB, SUB, 1)
     own_codes = own_codes.reshape(row_count // LANES, LANES, SUB).transpose(0, 2, 1)
     own_codes = own_codes.reshape(-1, LANES).astype(BF)
     spread = jnp.broadcast_to(own_codes[None], (n_ctx,) + own_codes.shape)
     all_codes = lax.all_to_all(spread, "ctx", 0, 0, tiled=True).astype(jnp.int32).reshape(-1, SUB, LANES)
-    meta = jnp.stack([own_first, kv]).astype(jnp.int32)
     attention, query_grad, books = attend(
-        meta,
         queries.reshape(-1, columns),
         grad_out.reshape(-1, columns),
         all_codes,

time: 72.5 us -> 69.6 us (0.960)
  blocking collectives: 38.2 us -> 58.2 us
  starting transfers between devices: 11.7 us -> 0 us
  waiting for transfers between devices: 8.95 us -> 0 us
  Pallas kernels: 10.6 us -> 9.16 us
    all_to_all x0 -> x1, blocking collectives: none -> 20.5 us  [per_device(): lax.all_to_all(spread, 'ctx', 0, 0, tiled=True).astype(jnp.int32)]
    all_to_all x1 -> x0, starting transfers between devices: 11.7 us -> none  [per_device(): lax.all_to_all(spread, 'ctx', 0, 0, tiled=True).astype(jnp.int32)]
    all_to_all x1 -> x0, waiting for transfers between devices: 8.95 us -> none  [per_device(): lax.all_to_all(spread, 'ctx', 0, 0, tiled=True).astype(jnp.int32)]
    pallas_call x1, Pallas kernels: 2.15 us -> 1.25 us  [finish(): pl.pallas_call(gather_sums, out_shape=(shape, shape), in_specs=[vm], out_...]
  transfers between devices with their start and end apart: 1 -> 0, of which waited for: 1 -> 0; matrix products, arithmetic and copies ran while one was open for 0% -> 0% of each run, Pallas kernels for 0% -> 0%
where the time goes in v3:
time: 69.6 us; the launch traced here: 69.4 us
  blocking collectives  58.2 us (84%)
  Pallas kernels  9.16 us (13%)
  local copies, waits for them, and re-layouts  1.18 us (2%)
  between operations  0.76 us (1%)
    all_to_all x1, blocking collectives, per_device(): lax.all_to_all(books.reshape(CODES, 2, columns), ('head', 'ctx'), 0, 0, t...  37.7 us
    all_to_all x1, blocking collectives, per_device(): lax.all_to_all(spread, 'ctx', 0, 0, tiled=True).astype(jnp.int32)  20.5 us
    pallas_call x1, Pallas kernels, attend(): pl.pallas_call(kernel, out_shape=(jax.ShapeDtypeStruct((rows, HD), BF), j...  7.91 us

profile of v3, /device:TPU:1, one launch (start us, length us, event | category | flops | bytes accessed | tf_op | source)
XLA Modules:
  0.0 69.4 jit_solution(13561078171003333447)
XLA Ops:
  0.6 0.0 copy-start
  0.7 0.9 %copy-done = s32[384,128]{1,0:T(8,128)S(1)} copy-done((s32[384,128]{1,0:T(8,128)S(1)}, s32[384,128]{1,0:T(8,128)}, u32[]{:S(2)}) %copy-start) | copy-done | bytes 196632
  1.6 0.1 constant_dynamic-slice_fusion
  1.7 0.0 copy-start.4
  1.7 0.1 copy.13
  1.8 0.0 copy-start.3
  1.8 0.0 copy-start.2
  1.9 0.0 copy-start.1
  1.9 20.5 %all_to_all.10 = bf16[16,48,128]{2,1,0:T(8,128)(2,1)S(1)} all-to-all(bf16[16,48,128]{2,1,0:T(8,128)(2,1)S(1)} %broadcast_in_dim.2), channel_id=1, replica_groups=mesh['ctx'=16,'head'=16] {'ctx'}, dimensions={0} | all-to-all | bytes 393216 | tf_op jit(solution)/shard_map/all_to_all | solution.py:253
  22.5 0.0 copy-done.4
  22.5 0.0 copy-done.3
  22.5 0.0 copy-done.2
  22.5 0.0 copy-done.1
  22.5 7.9 %shard_map.84 = (bf16[768,128]{1,0:T(8,128)(2,1)}, bf16[768,128]{1,0:T(8,128)(2,1)}, bf16[512,128]{1,0:T(8,128)(2,1)S(1)}) custom-call(bf16[768,128]{1,0:T(8,128)(2,1)S(1)} %bitcast.15, bf16[768,128]{1,0:T(8,128)(2,1)S(1)} %bitcast.16, s32[48,16,128]{2,1,0:T(8,128)S(1)} %convert.1.codes_ref, bf16[8,256,128]{2,1,0:T(8,128)(2,1)S(1)} %copy-done.1, ...), custom_call_target="tpu_custom_call" | custom-call | tf_op jit(solution)/shard_map/pallas_call | solution.py:186
  30.4 37.7 %all_to_all.11 = bf16[256,2,128]{2,1,0:T(2,128)(2,1)S(1)} all-to-all(bf16[256,2,128]{2,1,0:T(2,128)(2,1)S(1)} %bitcast.17), channel_id=1, replica_groups=mesh['ctx'=16,'head'=16] {'head','ctx'}, dimensions={0} | all-to-all | bytes 262144 | tf_op jit(solution)/shard_map/all_to_all | solution.py:261
  68.1 1.3 %shard_map.85 = (f32[8,8,16]{2,1,0:T(8,128)}, f32[8,8,16]{2,1,0:T(8,128)}) custom-call(bf16[512,128]{1,0:T(8,128)(2,1)S(1)} %bitcast.14), custom_call_target="tpu_custom_call" | custom-call | tf_op jit(solution)/shard_map/pallas_call | solution.py:236
  (5 shorter events, 0.1 us)
Async XLA Ops:
  0.6 0.9 %copy-start = (s32[384,128]{1,0:T(8,128)S(1)}, s32[384,128]{1,0:T(8,128)}, u32[]{:S(2)}) copy-start(s32[384,128]{1,0:T(8,128)} %param.6) | copy-start | bytes 589828
  1.7 20.8 %copy-start.4 = (bf16[384,2,128]{2,1,0:T(2,128)(2,1)S(1)}, bf16[384,2,128]{2,1,0:T(2,128)(2,1)}, u32[]{:S(2)}) copy-start(bf16[384,2,128]{2,1,0:T(2,128)(2,1)} %param.9) | copy-start | bytes 589828
  1.8 20.7 %copy-start.3 = (bf16[384,2,128]{2,1,0:T(2,128)(2,1)S(1)}, bf16[384,2,128]{2,1,0:T(2,128)(2,1)}, u32[]{:S(2)}) copy-start(bf16[384,2,128]{2,1,0:T(2,128)(2,1)} %param.5) | copy-start | bytes 589828
  1.8 20.7 %copy-start.2 = (bf16[8,256,128]{2,1,0:T(8,128)(2,1)S(1)}, bf16[8,256,128]{2,1,0:T(8,128)(2,1)}, u32[]{:S(2)}) copy-start(bf16[8,256,128]{2,1,0:T(8,128)(2,1)} %bv_ref.1) | copy-start | bytes 1572868
  1.9 20.6 %copy-start.1 = (bf16[8,256,128]{2,1,0:T(8,128)(2,1)S(1)}, bf16[8,256,128]{2,1,0:T(8,128)(2,1)}, u32[]{:S(2)}) copy-start(bf16[8,256,128]{2,1,0:T(8,128)(2,1)} %bk_ref.1) | copy-start | bytes 1572868

commit v4 on v3

--- a/solution.py
+++ b/solution.py
@@ -34,7 +34,7 @@
 
 
 def kernel(q_ref, g_ref, codes_ref, bk_ref, bv_ref, attn_ref, qg_ref, book_ref,
-           s_ref, kt_ref, vt_ref, next_ref, tk_ref, tv_ref, m_ref, l_ref, c_ref, o_ref, dq_ref, acc_ref,
+           s_ref, kt_ref, vt_ref, next_ref, tk_ref, tv_ref, m_ref, c_ref, o_ref, dq_ref, acc_ref,
            qt_ref, gt_ref, *bufs):
     rows = q_ref.shape[0]
     own_first = lax.axis_index("ctx") * (rows // HEADS)
@@ -47,8 +47,8 @@
     qt_ref[...] = q_ref[...].astype(F32).T.astype(BF)
     gt_ref[...] = g_ref[...].astype(F32).T.astype(BF)
     m_ref[...] = jnp.full((rows, LANES), NEGATIVE, F32)
-    l_ref[...] = jnp.zeros((rows, LANES), F32)
-    o_ref[...] = jnp.zeros((rows, HD), F32)
+    o_ref[...] = jnp.zeros((rows, 2 * HD), F32)
+    vt_ref[:, HD:] = jnp.ones((vt_ref.shape[0], HD, WIDE), BF)
 
     def decode(j, t_ref, out):
         for part in range(WIDE // LANES):
@@ -90,24 +90,21 @@
     lax.fori_loop(0, last, step_a, 0)
     scores(last, True)
     decode(0, tv_ref, next_ref)
-    vt_ref[0] = next_ref[...]
+    vt_ref[0, :HD] = next_ref[...]
     for c in chunks:
         m_ref[c] = jnp.broadcast_to(jnp.max(m_ref[c], axis=1, keepdims=True), (CHUNK, LANES))
 
     def step_b(j, more):
-        for c in chunks:
+        for c in [slice(0, rows)]:
             m = m_ref[c]
-            total = l_ref[c]
             es = []
             for p in range(0, WIDE, LANES):
                 e = jnp.exp2(s_ref[j, c, p:p + LANES] - m)
-                total = total + e
                 es.append(e)
-            l_ref[c] = total
             o_ref[c] += nt(jnp.concatenate(es, axis=1).astype(BF), vt_ref[j])
         if more:
             decode(j + 1, tv_ref, next_ref)
-            vt_ref[j + 1] = next_ref[...]
+            vt_ref[j + 1, :HD] = next_ref[...]
         return 0
 
     lax.fori_loop(0, last, lambda j, _: step_b(j, True), 0)
@@ -117,8 +114,8 @@
     for ref in (w_refs[-1], d_refs[-1], *x_refs[-2:]):
         ref[...] = jnp.zeros(ref.shape, BF)
     for c in chunks:
-        total = jnp.sum(l_ref[c], axis=1, keepdims=True)
-        out = (o_ref[c] / total).astype(BF)
+        total = o_ref[c, HD:]
+        out = (o_ref[c, :HD] / total).astype(BF)
         attn_ref[c] = out
         fix = jnp.sum(g_ref[c].astype(F32) * out.astype(F32), axis=1, keepdims=True)
         c_ref[c] = jnp.broadcast_to(fix, (CHUNK, LANES))
@@ -147,7 +144,7 @@
         for c in chunks:
             lse, fix = m_ref[c], c_ref[c]
             w = jnp.exp2(s_ref[j, c, parts[p]] - jnp.concatenate([lse] * (TILE // LANES), axis=1))
-            dp = nn(g_ref[c], vt_ref[j, :, parts[p]])
+            dp = nn(g_ref[c], vt_ref[j, :HD, parts[p]])
             w_refs[p][c] = w.astype(BF)
             d_refs[p][c] = (w * (dp - jnp.concatenate([fix] * (TILE // LANES), axis=1))).astype(BF)
 
@@ -192,14 +189,13 @@
         scratch_shapes=[
             pltpu.VMEM((tiles, rows, WIDE), F32),
             pltpu.VMEM((tiles, HD, WIDE), BF),
-            pltpu.VMEM((tiles, HD, WIDE), BF),
+            pltpu.VMEM((tiles, 2 * HD, WIDE), BF),
             pltpu.VMEM((HD, WIDE), BF),
             pltpu.VMEM((HD, CODES), F32),
             pltpu.VMEM((HD, CODES), F32),
             pltpu.VMEM((rows, LANES), F32),
             pltpu.VMEM((rows, LANES), F32),
-            pltpu.VMEM((rows, LANES), F32),
-            pltpu.VMEM((rows, HD), F32),
+            pltpu.VMEM((rows, 2 * HD), F32),
             pltpu.VMEM((rows, HD), F32),
             pltpu.VMEM((4, 256, 256), F32),
             pltpu.VMEM((HD, rows), BF),

time: 69.6 us -> 68.9 us (0.990)
  no operation moved by 1% of the time
where the time goes in v4:
time: 68.9 us; the launch traced here: 68.7 us
  blocking collectives  57.7 us (84%)
  Pallas kernels  8.98 us (13%)
  local copies, waits for them, and re-layouts  1.18 us (2%)
  between operations  0.76 us (1%)
    all_to_all x1, blocking collectives, per_device(): lax.all_to_all(books.reshape(CODES, 2, columns), ('head', 'ctx'), 0, 0, t...  37.2 us
    all_to_all x1, blocking collectives, per_device(): lax.all_to_all(spread, 'ctx', 0, 0, tiled=True).astype(jnp.int32)  20.5 us
    pallas_call x1, Pallas kernels, attend(): pl.pallas_call(kernel, out_shape=(jax.ShapeDtypeStruct((rows, HD), BF), j...  7.73 us

profile of v4, /device:TPU:1, one launch (start us, length us, event | category | flops | bytes accessed | tf_op | source)
XLA Modules:
  0.0 68.7 jit_solution(7856154781362297474)
XLA Ops:
  0.6 0.0 copy-start
  0.7 0.9 %copy-done = s32[384,128]{1,0:T(8,128)S(1)} copy-done((s32[384,128]{1,0:T(8,128)S(1)}, s32[384,128]{1,0:T(8,128)}, u32[]{:S(2)}) %copy-start) | copy-done | bytes 196632
  1.6 0.1 constant_dynamic-slice_fusion
  1.7 0.0 copy-start.4
  1.7 0.1 copy.13
  1.8 0.0 copy-start.3
  1.8 0.0 copy-start.2
  1.9 0.0 copy-start.1
  1.9 20.5 %all_to_all.10 = bf16[16,48,128]{2,1,0:T(8,128)(2,1)S(1)} all-to-all(bf16[16,48,128]{2,1,0:T(8,128)(2,1)S(1)} %broadcast_in_dim.2), channel_id=1, replica_groups=mesh['ctx'=16,'head'=16] {'ctx'}, dimensions={0} | all-to-all | bytes 393216 | tf_op jit(solution)/shard_map/all_to_all | solution.py:249
  22.5 0.0 copy-done.4
  22.5 0.0 copy-done.3
  22.5 0.0 copy-done.2
  22.5 0.0 copy-done.1
  22.5 7.7 %shard_map.84 = (bf16[768,128]{1,0:T(8,128)(2,1)}, bf16[768,128]{1,0:T(8,128)(2,1)}, bf16[512,128]{1,0:T(8,128)(2,1)S(1)}) custom-call(bf16[768,128]{1,0:T(8,128)(2,1)S(1)} %bitcast.15, bf16[768,128]{1,0:T(8,128)(2,1)S(1)} %bitcast.16, s32[48,16,128]{2,1,0:T(8,128)S(1)} %convert.1.codes_ref, bf16[8,256,128]{2,1,0:T(8,128)(2,1)S(1)} %copy-done.1, ...), custom_call_target="tpu_custom_call" | custom-call | tf_op jit(solution)/shard_map/pallas_call | solution.py:183
  30.3 37.2 %all_to_all.11 = bf16[256,2,128]{2,1,0:T(2,128)(2,1)S(1)} all-to-all(bf16[256,2,128]{2,1,0:T(2,128)(2,1)S(1)} %bitcast.17), channel_id=1, replica_groups=mesh['ctx'=16,'head'=16] {'head','ctx'}, dimensions={0} | all-to-all | bytes 262144 | tf_op jit(solution)/shard_map/all_to_all | solution.py:257
  67.5 1.3 %shard_map.85 = (f32[8,8,16]{2,1,0:T(8,128)}, f32[8,8,16]{2,1,0:T(8,128)}) custom-call(bf16[512,128]{1,0:T(8,128)(2,1)S(1)} %bitcast.14), custom_call_target="tpu_custom_call" | custom-call | tf_op jit(solution)/shard_map/pallas_call | solution.py:232
  (5 shorter events, 0.1 us)
Async XLA Ops:
  0.6 0.9 %copy-start = (s32[384,128]{1,0:T(8,128)S(1)}, s32[384,128]{1,0:T(8,128)}, u32[]{:S(2)}) copy-start(s32[384,128]{1,0:T(8,128)} %param.6) | copy-start | bytes 589828
  1.7 20.8 %copy-start.4 = (bf16[384,2,128]{2,1,0:T(2,128)(2,1)S(1)}, bf16[384,2,128]{2,1,0:T(2,128)(2,1)}, u32[]{:S(2)}) copy-start(bf16[384,2,128]{2,1,0:T(2,128)(2,1)} %param.9) | copy-start | bytes 589828
  1.8 20.7 %copy-start.3 = (bf16[384,2,128]{2,1,0:T(2,128)(2,1)S(1)}, bf16[384,2,128]{2,1,0:T(2,128)(2,1)}, u32[]{:S(2)}) copy-start(bf16[384,2,128]{2,1,0:T(2,128)(2,1)} %param.5) | copy-start | bytes 589828
  1.8 20.7 %copy-start.2 = (bf16[8,256,128]{2,1,0:T(8,128)(2,1)S(1)}, bf16[8,256,128]{2,1,0:T(8,128)(2,1)}, u32[]{:S(2)}) copy-start(bf16[8,256,128]{2,1,0:T(8,128)(2,1)} %bv_ref.1) | copy-start | bytes 1572868
  1.9 20.6 %copy-start.1 = (bf16[8,256,128]{2,1,0:T(8,128)(2,1)S(1)}, bf16[8,256,128]{2,1,0:T(8,128)(2,1)}, u32[]{:S(2)}) copy-start(bf16[8,256,128]{2,1,0:T(8,128)(2,1)} %bk_ref.1) | copy-start | bytes 1572868

commit v5 on v4

--- a/solution.py
+++ b/solution.py
@@ -4,7 +4,7 @@
 from jax import lax
 from jax.experimental import pallas as pl
 from jax.experimental.pallas import tpu as pltpu
-from jax.sharding import PartitionSpec as P
+from jax.sharding import Mesh, PartitionSpec as P
 
 KVH = 8
 HD = 128
@@ -38,7 +38,8 @@
            qt_ref, gt_ref, *bufs):
     rows = q_ref.shape[0]
     own_first = lax.axis_index("ctx") * (rows // HEADS)
-    kv = lax.axis_index("head") * HEADS // GROUP
+    kv = lax.axis_index("pair")
+    core = lax.axis_index("core")
     n_all = (own_first + rows // HEADS + WIDE - 1) // WIDE
     last = n_all - 1
     w_refs, d_refs, x_refs = bufs[:PARTS], bufs[PARTS:2 * PARTS], bufs[2 * PARTS:]
@@ -173,7 +174,8 @@
     for s in range(SUB):
         at = s % 4 * 64
         a = acc_ref[s // 4, at:at + 64, at:at + 64].astype(BF)
-        book_ref[s * 32:(s + 1) * 32] = jnp.concatenate([a[:32], a[32:]], axis=1)
+        to = (s + core) % 2 * CODES + s // 2 * 32
+        book_ref[pl.ds(pl.multiple_of(to, 32), 32)] = jnp.concatenate([a[:32], a[32:]], axis=1)
 
 
 def attend(q, g, codes, bk, bv):
@@ -240,8 +242,8 @@
 
 def per_device(queries, codes, codebook_k, codebook_v, grad_out):
     row_count, head_count, columns = queries.shape
-    n_ctx, n_head = lax.axis_size("ctx"), lax.axis_size("head")
-    kv = lax.axis_index("head") * head_count // GROUP
+    n_ctx = lax.axis_size("ctx")
+    kv = lax.axis_index("pair")
     own_codes = lax.dynamic_slice_in_dim(codes, kv * SUB, SUB, 1)
     own_codes = own_codes.reshape(row_count // LANES, LANES, SUB).transpose(0, 2, 1)
     own_codes = own_codes.reshape(-1, LANES).astype(BF)
@@ -254,8 +256,11 @@
         codebook_k,
         codebook_v,
     )
-    parts = lax.all_to_all(books.reshape(CODES, 2, columns), ("head", "ctx"), 0, 0, tiled=True)
-    sums_k, sums_v = finish(parts.reshape(books.shape))
+    own = books[:CODES]
+    other = lax.ppermute(books[CODES:], "core", [(0, 1), (1, 0)])
+    both = (own.astype(F32) + other.astype(F32)).astype(BF).reshape(CODES // 2, 2, columns)
+    parts = lax.all_to_all(both, ("pair", "ctx"), 0, 0, tiled=True)
+    sums_k, sums_v = finish(parts.reshape(own.shape))
     return (
         attention.reshape(queries.shape),
         query_grad.reshape(queries.shape),
@@ -265,16 +270,17 @@
 
 
 def solution(mesh):
-    placed = (P("ctx", "head", None), P("ctx", None), P(), P(), P("ctx", "head", None))
+    fine = Mesh(mesh.devices.reshape(mesh.devices.shape[0], -1, 2), ("ctx", "pair", "core"))
+    placed = (P("ctx", ("pair", "core"), None), P("ctx", None), P(), P(), P("ctx", ("pair", "core"), None))
     return jax.shard_map(
         per_device,
-        mesh=mesh,
+        mesh=fine,
         in_specs=placed,
         out_specs=(
-            P("ctx", "head", None),
-            P("ctx", "head", None),
-            P(None, "ctx", "head"),
-            P(None, "ctx", "head"),
+            P("ctx", ("pair", "core"), None),
+            P("ctx", ("pair", "core"), None),
+            P(None, "ctx", ("pair", "core")),
+            P(None, "ctx", ("pair", "core")),
         ),
         check_vma=False,
     )

time: 68.9 us -> 69.3 us (level)
  blocking collectives: 57.7 us -> 54.3 us
  starting transfers between devices: 0 us -> 2.44 us
  waiting for transfers between devices: 0 us -> 0.9 us
    all_to_all x1, blocking collectives: 37.2 us -> 33.8 us  [per_device(): parts = lax.all_to_all(both, ('pair', 'ctx'), 0, 0, tiled=True)]
    ppermute x0 -> x1, starting transfers between devices: none -> 2.44 us  [per_device(): other = lax.ppermute(books[CODES:], 'core', [(0, 1), (1, 0)])]
    ppermute x0 -> x1, waiting for transfers between devices: none -> 0.9 us  [per_device(): other = lax.ppermute(books[CODES:], 'core', [(0, 1), (1, 0)])]
  transfers between devices with their start and end apart: 0 -> 1, of which waited for: 0 -> 1; matrix products, arithmetic and copies ran while one was open for 0% -> 0% of each run, Pallas kernels for 0% -> 0%
where the time goes in v5:
time: 69.3 us; the launch traced here: 69.1 us
  blocking collectives  54.3 us (78%)
  Pallas kernels  9.44 us (14%)
  starting transfers between devices  2.44 us (4%)
  local copies, waits for them, and re-layouts  1.2 us (2%)
  waiting for transfers between devices  0.9 us (1%)
  between operations  0.75 us (1%)
    all_to_all x1, blocking collectives, per_device(): parts = lax.all_to_all(both, ('pair', 'ctx'), 0, 0, tiled=True)  33.8 us
    all_to_all x1, blocking collectives, per_device(): lax.all_to_all(spread, 'ctx', 0, 0, tiled=True).astype(jnp.int32)  20.5 us
    pallas_call x1, Pallas kernels, attend(): pl.pallas_call(kernel, out_shape=(jax.ShapeDtypeStruct((rows, HD), BF), j...  8.28 us
    ppermute x1, starting transfers between devices, per_device(): other = lax.ppermute(books[CODES:], 'core', [(0, 1), (1, 0)])  2.44 us
  transfers between devices with their start and end apart: 1, of which 1 were waited for; matrix products, arithmetic and copies ran while one was open for 0% of the time, Pallas kernels for 0%

profile of v5, /device:TPU:1, one launch (start us, length us, event | category | flops | bytes accessed | tf_op | source)
XLA Modules:
  0.0 69.1 jit_solution(3704812184948870672)
XLA Ops:
  0.6 0.0 copy-start
  0.7 0.9 %copy-done = s32[384,128]{1,0:T(8,128)S(1)} copy-done((s32[384,128]{1,0:T(8,128)S(1)}, s32[384,128]{1,0:T(8,128)}, u32[]{:S(2)}) %copy-start) | copy-done | bytes 196632
  1.6 0.1 constant_dynamic-slice_fusion
  1.7 0.0 copy-start.4
  1.7 0.1 copy.13
  1.8 0.0 copy-start.3
  1.8 0.0 copy-start.2
  1.9 0.0 copy-start.1
  1.9 20.5 %all_to_all.10 = bf16[16,48,128]{2,1,0:T(8,128)(2,1)S(1)} all-to-all(bf16[16,48,128]{2,1,0:T(8,128)(2,1)S(1)} %broadcast_in_dim.2), channel_id=1, replica_groups=mesh['ctx'=16,'pair'=8,'core'=2] {'ctx'}, dimensions={0} | all-to-all | bytes 393216 | tf_op jit(solution)/shard_map/all_to_all | solution.py:251
  22.5 0.0 copy-done.4
  22.5 0.0 copy-done.3
  22.5 0.0 copy-done.2
  22.5 0.0 copy-done.1
  22.5 8.3 %shard_map.84 = (bf16[768,128]{1,0:T(8,128)(2,1)}, bf16[768,128]{1,0:T(8,128)(2,1)}, bf16[512,128]{1,0:T(8,128)(2,1)S(1)}) custom-call(bf16[768,128]{1,0:T(8,128)(2,1)S(1)} %bitcast.15, bf16[768,128]{1,0:T(8,128)(2,1)S(1)} %bitcast.16, s32[48,16,128]{2,1,0:T(8,128)S(1)} %convert.1.codes_ref, bf16[8,256,128]{2,1,0:T(8,128)(2,1)S(1)} %copy-done.1, ...), custom_call_target="tpu_custom_call" | custom-call | tf_op jit(solution)/shard_map/pallas_call | solution.py:185
  30.8 2.4 %collective-permute-start = (bf16[256,128]{1,0:T(8,128)(2,1)S(1)}, bf16[256,128]{1,0:T(8,128)(2,1)S(1)}, u32[]{:S(2)}, u32[]{:S(2)}) collective-permute-start(bf16[256,128]{1,0:T(8,128)(2,1)S(1)} %slice.7), channel_id=1, source_target_pairs={{0,1},{1,0},{2,3},{3,2},{4,5},{5,4},{6,7},{7,6},{8,9},{9,8},{10,11... | collective-permute-start | bytes 196616 | tf_op jit(solution)/shard_map/ppermute | solution.py:260
  33.3 0.9 %collective-permute-done = bf16[256,128]{1,0:T(8,128)(2,1)S(1)} collective-permute-done((bf16[256,128]{1,0:T(8,128)(2,1)S(1)}, bf16[256,128]{1,0:T(8,128)(2,1)S(1)}, u32[]{:S(2)}, u32[]{:S(2)}) %collective-permute-start) | collective-permute-done | bytes 65568 | tf_op jit(solution)/shard_map/ppermute | solution.py:260
  34.2 33.8 %all_to_all.11 = bf16[128,2,128]{2,1,0:T(2,128)(2,1)S(1)} all-to-all(bf16[128,2,128]{2,1,0:T(2,128)(2,1)S(1)} %bitcast.18), channel_id=1, replica_groups=mesh['ctx'=16,'pair'=8,'core'=2] {'pair','ctx'}, dimensions={0} | all-to-all | bytes 131072 | tf_op jit(solution)/shard_map/all_to_all | solution.py:262
  68.0 1.2 %shard_map.85 = (f32[8,8,16]{2,1,0:T(8,128)}, f32[8,8,16]{2,1,0:T(8,128)}) custom-call(bf16[256,128]{1,0:T(8,128)(2,1)S(1)} %bitcast.14), custom_call_target="tpu_custom_call" | custom-call | tf_op jit(solution)/shard_map/pallas_call | solution.py:234
  (7 shorter events, 0.1 us)
Async XLA Ops:
  0.6 0.9 %copy-start = (s32[384,128]{1,0:T(8,128)S(1)}, s32[384,128]{1,0:T(8,128)}, u32[]{:S(2)}) copy-start(s32[384,128]{1,0:T(8,128)} %param.6) | copy-start | bytes 589828
  1.7 20.8 %copy-start.4 = (bf16[384,2,128]{2,1,0:T(2,128)(2,1)S(1)}, bf16[384,2,128]{2,1,0:T(2,128)(2,1)}, u32[]{:S(2)}) copy-start(bf16[384,2,128]{2,1,0:T(2,128)(2,1)} %param.9) | copy-start | bytes 589828
  1.8 20.7 %copy-start.3 = (bf16[384,2,128]{2,1,0:T(2,128)(2,1)S(1)}, bf16[384,2,128]{2,1,0:T(2,128)(2,1)}, u32[]{:S(2)}) copy-start(bf16[384,2,128]{2,1,0:T(2,128)(2,1)} %param.5) | copy-start | bytes 589828
  1.8 20.7 %copy-start.2 = (bf16[8,256,128]{2,1,0:T(8,128)(2,1)S(1)}, bf16[8,256,128]{2,1,0:T(8,128)(2,1)}, u32[]{:S(2)}) copy-start(bf16[8,256,128]{2,1,0:T(8,128)(2,1)} %bv_ref.1) | copy-start | bytes 1572868
  1.9 20.6 %copy-start.1 = (bf16[8,256,128]{2,1,0:T(8,128)(2,1)S(1)}, bf16[8,256,128]{2,1,0:T(8,128)(2,1)}, u32[]{:S(2)}) copy-start(bf16[8,256,128]{2,1,0:T(8,128)(2,1)} %bk_ref.1) | copy-start | bytes 1572868
  30.8 3.3 %collective-permute-start = (bf16[256,128]{1,0:T(8,128)(2,1)S(1)}, bf16[256,128]{1,0:T(8,128)(2,1)S(1)}, u32[]{:S(2)}, u32[]{:S(2)}) collective-permute-start(bf16[256,128]{1,0:T(8,128)(2,1)S(1)} %slice.7), channel_id=1, source_target_pairs={{0,1},{1,0},{2,3},{3,2},{4,5},{5,4},{6,7},{7,6},{8,9},{9,8},{10,11... | collective-permute-start | bytes 196616 | tf_op jit(solution)/shard_map/ppermute | solution.py:260

commit v6 on v4

--- a/solution.py
+++ b/solution.py
@@ -62,11 +62,12 @@
                 b = jnp.take_along_axis(t_ref[r, LANES:], low, axis=1, mode="promise_in_bounds")
                 out[r, part * LANES:(part + 1) * LANES] = jnp.where(upper, b, a).astype(BF)
 
+    whole = [slice(0, rows)]
     chunks = [slice(c, c + CHUNK) for c in range(0, rows, CHUNK)]
     parts = [slice(p * TILE, (p + 1) * TILE) for p in range(PARTS)]
 
     def scores(j, masked):
-        for c in chunks:
+        for c in whole:
             top = m_ref[c]
             for p in parts:
                 s = nn(q_ref[c], kt_ref[j, :, p]) * (SCALE * LOG2E)
@@ -95,7 +96,7 @@
         m_ref[c] = jnp.broadcast_to(jnp.max(m_ref[c], axis=1, keepdims=True), (CHUNK, LANES))
 
     def step_b(j, more):
-        for c in [slice(0, rows)]:
+        for c in whole:
             m = m_ref[c]
             es = []
             for p in range(0, WIDE, LANES):
@@ -118,7 +119,13 @@
         out = (o_ref[c, :HD] / total).astype(BF)
         attn_ref[c] = out
         fix = jnp.sum(g_ref[c].astype(F32) * out.astype(F32), axis=1, keepdims=True)
-        c_ref[c] = jnp.broadcast_to(fix, (CHUNK, LANES))
+        fix = jnp.broadcast_to(-fix, (CHUNK, LANES))
+        lane = lax.broadcasted_iota(jnp.int32, fix.shape, 1)
+        first = fix.astype(BF).astype(F32)
+        second = (fix - first).astype(BF).astype(F32)
+        third = fix - first - second
+        terms = jnp.where(lane == 0, first, jnp.where(lane == 1, second, jnp.where(lane == 2, third, 0.0)))
+        c_ref[c] = jnp.concatenate([g_ref[c], terms.astype(BF)], axis=1)
         m_ref[c] = m_ref[c] + jnp.log2(total)
 
     hi_iota = lax.broadcasted_iota(jnp.int32, (64, TILE), 0).astype(F32).astype(BF)
@@ -141,12 +148,12 @@
             acc_ref[grp] += nt(jnp.concatenate(his, axis=0), jnp.concatenate(xs, axis=0))
 
     def slopes(j, p):
-        for c in chunks:
-            lse, fix = m_ref[c], c_ref[c]
+        for c in whole:
+            lse = m_ref[c]
             w = jnp.exp2(s_ref[j, c, parts[p]] - jnp.concatenate([lse] * (TILE // LANES), axis=1))
-            dp = nn(g_ref[c], vt_ref[j, :HD, parts[p]])
+            dp = nn(c_ref[c], vt_ref[j, :, parts[p]])
             w_refs[p][c] = w.astype(BF)
-            d_refs[p][c] = (w * (dp - jnp.concatenate([fix] * (TILE // LANES), axis=1))).astype(BF)
+            d_refs[p][c] = (w * dp).astype(BF)
 
     def products(j, p):
         for c in chunks:
@@ -194,7 +201,7 @@
             pltpu.VMEM((HD, CODES), F32),
             pltpu.VMEM((HD, CODES), F32),
             pltpu.VMEM((rows, LANES), F32),
-            pltpu.VMEM((rows, LANES), F32),
+            pltpu.VMEM((rows, 2 * HD), BF),
             pltpu.VMEM((rows, 2 * HD), F32),
             pltpu.VMEM((rows, HD), F32),
             pltpu.VMEM((4, 256, 256), F32),

time: 68.9 us -> 68.9 us (level)
  no operation moved by 1% of the time
where the time goes in v6:
time: 68.9 us; the launch traced here: 68.7 us
  blocking collectives  57.8 us (84%)
  Pallas kernels  8.97 us (13%)
  local copies, waits for them, and re-layouts  1.18 us (2%)
  between operations  0.76 us (1%)
    all_to_all x1, blocking collectives, per_device(): lax.all_to_all(books.reshape(CODES, 2, columns), ('head', 'ctx'), 0, 0, t...  37.2 us
    all_to_all x1, blocking collectives, per_device(): lax.all_to_all(spread, 'ctx', 0, 0, tiled=True).astype(jnp.int32)  20.5 us
    pallas_call x1, Pallas kernels, attend(): pl.pallas_call(kernel, out_shape=(jax.ShapeDtypeStruct((rows, HD), BF), j...  7.72 us

profile of v6, /device:TPU:1, one launch (start us, length us, event | category | flops | bytes accessed | tf_op | source)
XLA Modules:
  0.0 68.7 jit_solution(13061823112813667032)
XLA Ops:
  0.6 0.0 copy-start
  0.7 0.9 %copy-done = s32[384,128]{1,0:T(8,128)S(1)} copy-done((s32[384,128]{1,0:T(8,128)S(1)}, s32[384,128]{1,0:T(8,128)}, u32[]{:S(2)}) %copy-start) | copy-done | bytes 196632
  1.6 0.1 constant_dynamic-slice_fusion
  1.7 0.0 copy-start.4
  1.7 0.1 copy.13
  1.8 0.0 copy-start.3
  1.8 0.0 copy-start.2
  1.9 0.0 copy-start.1
  1.9 20.5 %all_to_all.10 = bf16[16,48,128]{2,1,0:T(8,128)(2,1)S(1)} all-to-all(bf16[16,48,128]{2,1,0:T(8,128)(2,1)S(1)} %broadcast_in_dim.2), channel_id=1, replica_groups=mesh['ctx'=16,'head'=16] {'ctx'}, dimensions={0} | all-to-all | bytes 393216 | tf_op jit(solution)/shard_map/all_to_all | solution.py:256
  22.5 0.0 copy-done.4
  22.5 0.0 copy-done.3
  22.5 0.0 copy-done.2
  22.5 0.0 copy-done.1
  22.5 7.7 %shard_map.84 = (bf16[768,128]{1,0:T(8,128)(2,1)}, bf16[768,128]{1,0:T(8,128)(2,1)}, bf16[512,128]{1,0:T(8,128)(2,1)S(1)}) custom-call(bf16[768,128]{1,0:T(8,128)(2,1)S(1)} %bitcast.15, bf16[768,128]{1,0:T(8,128)(2,1)S(1)} %bitcast.16, s32[48,16,128]{2,1,0:T(8,128)S(1)} %convert.1.codes_ref, bf16[8,256,128]{2,1,0:T(8,128)(2,1)S(1)} %copy-done.1, ...), custom_call_target="tpu_custom_call" | custom-call | tf_op jit(solution)/shard_map/pallas_call | solution.py:190
  30.2 37.2 %all_to_all.11 = bf16[256,2,128]{2,1,0:T(2,128)(2,1)S(1)} all-to-all(bf16[256,2,128]{2,1,0:T(2,128)(2,1)S(1)} %bitcast.17), channel_id=1, replica_groups=mesh['ctx'=16,'head'=16] {'head','ctx'}, dimensions={0} | all-to-all | bytes 262144 | tf_op jit(solution)/shard_map/all_to_all | solution.py:264
  67.5 1.2 %shard_map.85 = (f32[8,8,16]{2,1,0:T(8,128)}, f32[8,8,16]{2,1,0:T(8,128)}) custom-call(bf16[512,128]{1,0:T(8,128)(2,1)S(1)} %bitcast.14), custom_call_target="tpu_custom_call" | custom-call | tf_op jit(solution)/shard_map/pallas_call | solution.py:239
  (5 shorter events, 0.1 us)
Async XLA Ops:
  0.6 0.9 %copy-start = (s32[384,128]{1,0:T(8,128)S(1)}, s32[384,128]{1,0:T(8,128)}, u32[]{:S(2)}) copy-start(s32[384,128]{1,0:T(8,128)} %param.6) | copy-start | bytes 589828
  1.7 20.8 %copy-start.4 = (bf16[384,2,128]{2,1,0:T(2,128)(2,1)S(1)}, bf16[384,2,128]{2,1,0:T(2,128)(2,1)}, u32[]{:S(2)}) copy-start(bf16[384,2,128]{2,1,0:T(2,128)(2,1)} %param.9) | copy-start | bytes 589828
  1.8 20.7 %copy-start.3 = (bf16[384,2,128]{2,1,0:T(2,128)(2,1)S(1)}, bf16[384,2,128]{2,1,0:T(2,128)(2,1)}, u32[]{:S(2)}) copy-start(bf16[384,2,128]{2,1,0:T(2,128)(2,1)} %param.5) | copy-start | bytes 589828
  1.8 20.7 %copy-start.2 = (bf16[8,256,128]{2,1,0:T(8,128)(2,1)S(1)}, bf16[8,256,128]{2,1,0:T(8,128)(2,1)}, u32[]{:S(2)}) copy-start(bf16[8,256,128]{2,1,0:T(8,128)(2,1)} %bv_ref.1) | copy-start | bytes 1572868
  1.9 20.6 %copy-start.1 = (bf16[8,256,128]{2,1,0:T(8,128)(2,1)S(1)}, bf16[8,256,128]{2,1,0:T(8,128)(2,1)}, u32[]{:S(2)}) copy-start(bf16[8,256,128]{2,1,0:T(8,128)(2,1)} %bk_ref.1) | copy-start | bytes 1572868
